TPU v7x, 512 devices: a whole 4x4x16 slice. The times are simulated.
512 devices in a mesh: ch: 4 (over z_hi, core), gr: 16 (over x, y), gc: 8 (over z_lo).
Axes of the slice: x: 4, y: 4, z: 16 (z_hi: 2, z_lo: 8; z = z_hi * 8 + z_lo), core: 2. Of those that a mesh axis runs over, the one named last changes fastest.
Arguments:
- features: bfloat16 [3, 16384, 8192], P(None, ('gr', 'gc'), 'ch'), may hold values from -6 to 6
- short_taps: float32 [3, 7, 8192], P(None, None, 'ch'), may hold values from -2 to 2
- decay: float32 [16, 8192], P(None, 'ch'), may hold values from 1.5258789e-05 to 0.1, as said below
- residue: float32 [16, 8192], P(None, 'ch'), may hold values from -1 to 1
- doc_lengths: int32 [8], replicated, may hold values from 1 to 4096, 16384 in all
- gain: float32 [8192], P('ch'), may hold values from 0.5 to 1.5
Outputs:
- mixed: bfloat16 [16384, 8192], P(('gr', 'gc'), 'ch')
Inputs may be any that keep to these rules, and one draw needn't show every extreme that they name: `doc_lengths`: positive lengths summing to 16384; the largest equals the stated maximum. Positive decay rates.
All inputs are finite; a program needn't handle non-finite values.
Results may differ from a plain program's by a relative error of at most 0.0077.
Values may be sent and summed in bfloat16 or wider, within the bound.
No kernel may reach another device: no remote copies, remote signals or barrier semaphores. Data moves between devices by JAX's collectives and lax.ppermute only.
A program may use at most 128 MiB of HBM per device.

v0:
```python
import math

import jax
import jax.numpy as jnp
from jax import lax
from jax.sharding import PartitionSpec as P

highest_mode = lax.Precision.HIGHEST


def passed_along(block, axis, distance):
    devices = range(lax.axis_size(axis))
    route = [(i - distance, i) for i in devices if i - distance in devices]
    return lax.ppermute(block, axis, route)


def angle_of(left, right, modulus):
    return 2.0 * math.pi / modulus * (left * right % modulus).astype(jnp.float32)


def spin(table_pair, values):
    return jnp.einsum("tkj,rqjc->trqkc", table_pair, values, precision=highest_mode)


def regroup(block):
    planes, groups, extent = block.shape
    moved = lax.all_to_all(
        block.reshape(planes, groups, 1, extent),
        ("gr", "gc"),
        split_axis=1,
        concat_axis=2,
        tiled=True,
    )
    return moved.reshape(planes, groups, extent)


def fft_conv(mixed_in, decay, residue):
    tokens, channels = mixed_in.shape
    groups = lax.axis_size(("gr", "gc"))
    per_group = tokens // groups
    here = lax.axis_index(("gr", "gc"))
    length = groups * tokens
    period = 2 * length
    freq_rows = 2 * groups
    received = lax.all_to_all(
        mixed_in.reshape(1, groups, 1, per_group * channels),
        ("gr", "gc"),
        split_axis=1,
        concat_axis=2,
        tiled=True,
    )
    columns = received.reshape(groups, per_group * channels).astype(jnp.float32)
    source = jnp.arange(groups, dtype=jnp.int32)
    freq_index = jnp.arange(freq_rows, dtype=jnp.int32)
    phase = angle_of(freq_index[:, None], source[None, :], freq_rows)
    first_table = jnp.concatenate([jnp.cos(phase), -jnp.sin(phase)], axis=0)
    first_both = jnp.dot(first_table, columns, precision=highest_mode).reshape(
        2, freq_rows, per_group, channels
    )
    first_re = first_both[0]
    first_im = first_both[1]
    column_pos = here * per_group + jnp.arange(per_group, dtype=jnp.int32)
    twist = angle_of(freq_index[:, None], column_pos[None, :], period)
    twist_cos = jnp.cos(twist)[:, :, None]
    twist_sin = jnp.sin(twist)[:, :, None]
    turned_re = first_re * twist_cos + first_im * twist_sin
    turned_im = first_im * twist_cos - first_re * twist_sin
    stacked = jnp.stack([turned_re, turned_im]).reshape(4, groups, per_group * channels)
    spectrum_rows = regroup(stacked).reshape(2, 2, tokens, channels)
    inner = jnp.arange(tokens, dtype=jnp.int32)
    wave = angle_of(inner[:, None], inner[None, :], tokens)
    wave_pair = jnp.stack([jnp.cos(wave), jnp.sin(wave)])
    forward = spin(wave_pair, spectrum_rows)
    spec_re = forward[0, 0] + forward[1, 1]
    spec_im = forward[0, 1] - forward[1, 0]
    freq_low = jnp.arange(2, dtype=jnp.int32) * groups + here
    frequency = freq_low[:, None] + freq_rows * inner[None, :]
    half_turn = math.pi / period * frequency.astype(jnp.float32)
    sine_half = jnp.sin(half_turn)
    sine_full = jnp.sin(2.0 * half_turn)
    parity = 1.0 - 2.0 * (frequency % 2).astype(jnp.float32)
    rates = decay[:, None, None, :]
    weights = residue[:, None, None, :]
    ratio = jnp.exp(-rates)
    numer = 1.0 - jnp.exp(-rates * length) * parity[None, :, :, None]
    real_den = -jnp.expm1(-rates) + 2.0 * ratio * (sine_half * sine_half)[None, :, :, None]
    imag_den = ratio * sine_full[None, :, :, None]
    factor = weights * jnp.sqrt(2.0 * rates) * numer / (real_den * real_den + imag_den * imag_den)
    filt_re = jnp.sum(factor * real_den, axis=0)
    filt_im = -jnp.sum(factor * imag_den, axis=0)
    prod_re = spec_re * filt_re - spec_im * filt_im
    prod_im = spec_re * filt_im + spec_im * filt_re
    backward = spin(wave_pair, jnp.stack([prod_re, prod_im]))
    back_re = backward[0, 0] - backward[1, 1]
    back_im = backward[0, 1] + backward[1, 0]
    rotate = angle_of(freq_low[:, None], inner[None, :], period)
    rotate_cos = jnp.cos(rotate)[:, :, None]
    rotate_sin = jnp.sin(rotate)[:, :, None]
    final_re = back_re * rotate_cos - back_im * rotate_sin
    final_im = back_re * rotate_sin + back_im * rotate_cos
    outgoing = jnp.stack([final_re, final_im]).reshape(4, groups, per_group * channels)
    arrived = regroup(outgoing).reshape(2 * freq_rows, per_group * channels)
    back_phase = angle_of(source[:, None], freq_index[None, :], freq_rows)
    back_table = jnp.concatenate([jnp.cos(back_phase), -jnp.sin(back_phase)], axis=1)
    result = jnp.dot(back_table, arrived, precision=highest_mode) / period
    conv_out = result.astype(jnp.bfloat16).reshape(1, groups, 1, per_group * channels)
    return lax.all_to_all(conv_out, ("gr", "gc"), split_axis=1, concat_axis=2, tiled=True).reshape(
        tokens, channels
    )


def per_device(features, short_taps, decay, residue, doc_lengths, gain):
    planes, tokens, channels = features.shape
    here = lax.axis_index(("gr", "gc"))
    before = passed_along(features[:, tokens - 6 :, :], ("gr", "gc"), 1)
    extended = jnp.concatenate([before, features], axis=1)
    starts = jnp.cumsum(doc_lengths) - doc_lengths
    position = here * tokens + jnp.arange(tokens, dtype=jnp.int32)
    begins = jnp.max(jnp.where(starts[None, :] <= position[:, None], starts[None, :], 0), axis=1)
    reach = position - begins
    summed = jnp.zeros((planes, tokens, channels), jnp.float32)
    for offset in range(7):
        window = extended[:, 6 - offset : 6 - offset + tokens, :].astype(jnp.float32)
        summed = summed + jnp.where(
            (reach >= offset)[None, :, None], short_taps[:, offset, None, :] * window, 0.0
        )
    featured = summed.astype(jnp.bfloat16)
    mixed_in = (featured[0].astype(jnp.float32) * featured[2].astype(jnp.float32)).astype(
        jnp.bfloat16
    )
    returned = fft_conv(mixed_in, decay, residue)
    gated = featured[1].astype(jnp.float32) * returned.astype(jnp.float32)
    energy = lax.psum(jnp.sum(gated * gated, axis=1), "ch")
    width_total = channels * lax.axis_size("ch")
    scaling = lax.rsqrt(energy / width_total + 1e-06)
    return (gated * scaling[:, None] * gain[None, :]).astype(jnp.bfloat16)


def solution(mesh):
    placed = (
        P(None, ("gr", "gc"), "ch"),
        P(None, None, "ch"),
        P(None, "ch"),
        P(None, "ch"),
        P(),
        P("ch"),
    )
    return jax.shard_map(
        per_device, mesh=mesh, in_specs=placed, out_specs=P(("gr", "gc"), "ch"), check_vma=False
    )
```

profile of v0, /device:TPU:32, one launch (start us, length us, event | category | flops | bytes accessed | tf_op | source)
XLA Modules:
  0.0 584.0 jit_solution(6454468070856112287)
XLA Ops:
  0.0 0.9 slice.85
  0.9 3.8 collective-permute-start
  4.8 0.8 reduce-window.9
  5.6 0.7 bitcast_subtract_fusion
  6.4 2.3 fusion.77
  8.8 1.5 collective-permute-done
  10.3 9.9 %add_convert_fusion = bf16[3,128,2048]{2,1,0:T(8,128)(2,1)S(1)} fusion(bf16[3,128,2048]{2,1,0:T(8,128)(2,1)} %param.6, bf16[3,6,2048]{2,1,0:T(8,128)(2,1)S(1)} %collective-permute-done, f32[3,2048]{1,0:T(4,128)S(1)} %get-tuple-element.38, f32[3,2048]{1,0:T(4,128)S(1)} %get-tuple-element.39, f32[3,2048]{1,0:T(4,128)S(1)} %get-tuple-element.40, ...), kind=kLoop, calls=%fused_computation.19 | loop fusion | flops 36175872 | bytes 3392384 | tf_op jit(solution)/shard_map/convert_element_type | solution.py:127
  20.2 0.1 fusion.20
  20.3 0.8 copy.84
  21.1 0.6 broadcast.498
  21.7 3.7 reduce
  25.4 1.2 reshape.608
  26.6 16.8 %all-to-all-start = ((bf16[128,2,1024]{2,1,0:T(2,128)(2,1)}), bf16[128,2,1024]{2,1,0:T(2,128)(2,1)S(1)}, u32[]{:S(2)}, u32[]{:S(2)}) async-start(bf16[128,2,1024]{2,1,0:T(2,128)(2,1)} %reshape.608), calls=%async_computation | async-start | bytes 1048576 | tf_op jit(solution)/shard_map/all_to_all | solution.py:45
  43.5 0.5 sine_negate_fusion
  44.0 29.9 %all-to-all-done = bf16[128,2,1024]{2,1,0:T(2,128)(2,1)S(1)} async-done(((bf16[128,2,1024]{2,1,0:T(2,128)(2,1)}), bf16[128,2,1024]{2,1,0:T(2,128)(2,1)S(1)}, u32[]{:S(2)}, u32[]{:S(2)}) %all-to-all-start) | async-done | bytes 524320 | tf_op jit(solution)/shard_map/all_to_all | solution.py:45
  73.9 0.4 reshape.609
  74.3 1.8 fusion.21
  76.2 0.7 add_bitcast_fusion
  76.9 0.4 pad_maximum_fusion
  77.3 4.7 copy.40
  81.9 10.4 %all-to-all-start.1 = ((f32[4,128,1,2048]{3,0,2,1:T(4,128)}), f32[4,128,1,2048]{3,0,2,1:T(4,128)}, u32[]{:S(2)}, u32[]{:S(2)}) async-start(f32[4,128,1,2048]{3,0,2,1:T(4,128)} %copy.40), calls=%async_computation.1 | async-start | bytes 8388608 | tf_op jit(solution)/shard_map/all_to_all | solution.py:27
  92.3 0.1 fusion.60
  92.5 0.1 sqrt_multiply_fusion
  92.6 20.5 %fusion.2 = (f32[2,128,2048]{2,1,0:T(8,128)}, f32[2,128,2048]{2,1,0:T(8,128)}) fusion(f32[2,128]{1,0:T(2,128)S(1)} %get-tuple-element.29, f32[16,2048]{1,0:T(8,128)S(1)} %get-tuple-element.25, f32[2,128]{1,0:T(2,128)S(1)} %get-tuple-element.28, f32[16,2048]{1,0:T(8,128)S(1)} %get-tuple-element.23, f32[16,2048]{1,0:T(8,128)S(1)} %get-tuple-element.24, ...), kind=kLoop, calls=%fused_computation.4 | loop fusion | flops 116391936 | bytes 4852736 | tf_op jit(solution)/shard_map/reduce_sum | solution.py:90
  113.1 2.9 copy.44
  116.0 2.9 copy.45
  118.9 0.3 fusion.50
  119.1 157.7 %all-to-all-done.1 = f32[4,128,1,2048]{3,0,2,1:T(4,128)} async-done(((f32[4,128,1,2048]{3,0,2,1:T(4,128)}), f32[4,128,1,2048]{3,0,2,1:T(4,128)}, u32[]{:S(2)}, u32[]{:S(2)}) %all-to-all-start.1) | async-done | bytes 4194336 | tf_op jit(solution)/shard_map/all_to_all | solution.py:27
  276.8 5.3 copy.41
  282.2 9.1 %convolution_bitcast_fusion.1 = f32[2,2,2,128,2048]{3,4,0,2,1:T(8,128)S(1)} fusion(f32[2,2,128,2048,1]{2,3,4,1,0:T(8,128)} %bitcast.147, f32[1,128,128]{2,1,0:T(8,128)S(1)} %get-tuple-element.48, f32[1,128,128]{2,1,0:T(8,128)S(1)} %get-tuple-element.49), kind=kOutput, calls=%fused_computation.8 | convolution fusion | flops 3221258240 | bytes 12713984 | tf_op jit(solution)/shard_map/tkj,rqjc->trqkc/dot_general | solution.py:22
  291.4 0.6 fusion.13
  292.0 6.8 %convolution_bitcast_fusion = f32[2,2,2,128,2048]{3,4,0,2,1:T(8,128)S(1)} fusion(f32[1,2,128,2048]{2,3,1,0:T(8,128)S(1)} %get-tuple-element.10, f32[1,2,128,2048]{2,3,1,0:T(8,128)S(1)} %get-tuple-element.9, f32[1,128,128]{2,1,0:T(8,128)S(1)} %get-tuple-element.48, f32[1,128,128]{2,1,0:T(8,128)S(1)} %get-tuple-element.49), kind=kOutput, calls=%fused_computation.7 | convolution fusion | flops 3222306816 | bytes 12713984 | tf_op jit(solution)/shard_map/tkj,rqjc->trqkc/dot_general | solution.py:22
  298.7 0.6 multiply_subtract_fusion
  299.4 2.2 pad_maximum_fusion.1
  301.6 5.5 copy.48
  307.1 11.5 %all-to-all-start.2 = ((f32[4,128,1,2048]{3,0,2,1:T(4,128)}), f32[4,128,1,2048]{3,0,2,1:T(4,128)}, u32[]{:S(2)}, u32[]{:S(2)}) async-start(f32[4,128,1,2048]{3,0,2,1:T(4,128)} %copy.48), calls=%async_computation.2 | async-start | bytes 8388608 | tf_op jit(solution)/shard_map/all_to_all | solution.py:27
  318.6 0.5 sine_negate_fusion.1
  319.1 184.8 %all-to-all-done.2 = f32[4,128,1,2048]{3,0,2,1:T(4,128)} async-done(((f32[4,128,1,2048]{3,0,2,1:T(4,128)}), f32[4,128,1,2048]{3,0,2,1:T(4,128)}, u32[]{:S(2)}, u32[]{:S(2)}) %all-to-all-start.2) | async-done | bytes 4194336 | tf_op jit(solution)/shard_map/all_to_all | solution.py:27
  503.9 4.6 copy.49
  508.5 2.3 fusion.6
  510.8 0.8 copy.83
  511.7 3.7 reduce.1
  515.4 0.4 reshape.610
  515.8 41.4 %all_to_all.16 = bf16[128,2,1024]{2,1,0:T(2,128)(2,1)S(1)} all-to-all(bf16[128,2,1024]{2,1,0:T(2,128)(2,1)S(1)} %reshape.610), channel_id=1, replica_groups=mesh['ch'=4,'gr'=16,'gc'=8] {'gr','gc'}, dimensions={0} | all-to-all | bytes 1048576 | tf_op jit(solution)/shard_map/all_to_all | solution.py:107
  557.2 0.4 reshape.611
  557.6 0.6 multiply_reduce_fusion.1
  558.2 24.1 %psum.7 = f32[128]{0:T(128)S(1)} all-reduce(f32[128]{0:T(128)S(1)} %multiply_reduce_fusion.1), channel_id=1, replica_groups=mesh['ch'=4,'gr'=16,'gc'=8] {'ch'}, use_global_device_ids=true, to_apply=%region_5.6 | all-reduce | flops 128 | bytes 1024 | tf_op jit(solution)/shard_map/psum | solution.py:133
  582.3 1.3 multiply_convert_fusion
  (22 shorter events, 0.3 us)
Async XLA Ops:
  0.9 9.4 %collective-permute-start = (bf16[3,6,2048]{2,1,0:T(8,128)(2,1)S(1)}, bf16[3,6,2048]{2,1,0:T(8,128)(2,1)S(1)}, u32[]{:S(2)}, u32[]{:S(2)}) collective-permute-start(bf16[3,6,2048]{2,1,0:T(8,128)(2,1)S(1)} %slice.85), channel_id=1, source_target_pairs={{0,1},{1,2},{2,3},{3,4},{4,5},{5,6},{6,7},{7,8},{8,9},{9,10},{10,1... | collective-permute-start | bytes 221192 | tf_op jit(solution)/shard_map/ppermute | solution.py:14
  26.6 47.3 %all-to-all-start = ((bf16[128,2,1024]{2,1,0:T(2,128)(2,1)}), bf16[128,2,1024]{2,1,0:T(2,128)(2,1)S(1)}, u32[]{:S(2)}, u32[]{:S(2)}) async-start(bf16[128,2,1024]{2,1,0:T(2,128)(2,1)} %reshape.608), calls=%async_computation | async-start | bytes 1048576 | tf_op jit(solution)/shard_map/all_to_all | solution.py:45
  81.9 10.5 %copy-start.2 = (f32[16,2048]{1,0:T(8,128)S(1)}, f32[16,2048]{1,0:T(8,128)}, u32[]{:S(2)}) copy-start(f32[16,2048]{1,0:T(8,128)} %param.9) | copy-start | bytes 393220
  81.9 10.6 %copy-start.3 = (f32[16,2048]{1,0:T(8,128)S(1)}, f32[16,2048]{1,0:T(8,128)}, u32[]{:S(2)}) copy-start(f32[16,2048]{1,0:T(8,128)} %param.8) | copy-start | bytes 393220
  81.9 194.9 %all-to-all-start.1 = ((f32[4,128,1,2048]{3,0,2,1:T(4,128)}), f32[4,128,1,2048]{3,0,2,1:T(4,128)}, u32[]{:S(2)}, u32[]{:S(2)}) async-start(f32[4,128,1,2048]{3,0,2,1:T(4,128)} %copy.40), calls=%async_computation.1 | async-start | bytes 8388608 | tf_op jit(solution)/shard_map/all_to_all | solution.py:27
  282.2 9.2 %copy-start = (f32[2,128,2048]{1,2,0:T(8,128)S(1)}, f32[2,128,2048]{1,2,0:T(8,128)}, u32[]{:S(2)}) copy-start(f32[2,128,2048]{1,2,0:T(8,128)} %copy.44) | copy-start | bytes 6291460
  282.2 9.2 %copy-start.1 = (f32[2,128,2048]{1,2,0:T(8,128)S(1)}, f32[2,128,2048]{1,2,0:T(8,128)}, u32[]{:S(2)}) copy-start(f32[2,128,2048]{1,2,0:T(8,128)} %copy.45) | copy-start | bytes 6291460
  307.1 196.8 %all-to-all-start.2 = ((f32[4,128,1,2048]{3,0,2,1:T(4,128)}), f32[4,128,1,2048]{3,0,2,1:T(4,128)}, u32[]{:S(2)}, u32[]{:S(2)}) async-start(f32[4,128,1,2048]{3,0,2,1:T(4,128)} %copy.48), calls=%async_computation.2 | async-start | bytes 8388608 | tf_op jit(solution)/shard_map/all_to_all | solution.py:27
  511.7 70.6 %copy-start.4 = (f32[2048]{0:T(1024)S(1)}, f32[2048]{0:T(1024)}, u32[]{:S(2)}) copy-start(f32[2048]{0:T(1024)} %param.11) | copy-start | bytes 24580
where the time goes:
time: 592 us; the launch traced here: 584 us
  waiting for transfers between devices  374 us (63%)
  blocking collectives  65.5 us (11%)
  other arithmetic  47.5 us (8%)
  starting transfers between devices  42.5 us (7%)
  local copies, waits for them, and re-layouts  33.8 us (6%)
  matrix products  20.1 us (3%)
    all_to_all x2, waiting for transfers between devices, regroup(): lax.all_to_all(block.reshape(planes, groups, 1, extent), ('gr', 'gc'), sp...  342 us
    all_to_all x1, blocking collectives, fft_conv(): lax.all_to_all(conv_out, ('gr', 'gc'), split_axis=1, concat_axis=2, tiled...  41.4 us
    all_to_all x1, waiting for transfers between devices, fft_conv(): lax.all_to_all(mixed_in.reshape(1, groups, 1, per_group * channels), ('gr...  29.9 us
    psum x1, blocking collectives, per_device(): energy = lax.psum(jnp.sum(gated * gated, axis=1), 'ch')  24.1 us
    all_to_all x2, starting transfers between devices, regroup(): lax.all_to_all(block.reshape(planes, groups, 1, extent), ('gr', 'gc'), sp...  21.9 us
    reduce_sum x1, other arithmetic, fft_conv(): filt_im = -jnp.sum(factor * imag_den, axis=0)  20.5 us
    all_to_all x1, starting transfers between devices, fft_conv(): lax.all_to_all(mixed_in.reshape(1, groups, 1, per_group * channels), ('gr...  16.8 us
    dot_general x2, matrix products, spin(): jnp.einsum('tkj,rqjc->trqkc', table_pair, values, precision=highest_mode)  15.9 us
  transfers between devices with their start and end apart: 4, of which 4 were waited for; matrix products, arithmetic and copies ran while one was open for 5% of the time, Pallas kernels for 0%

commit v1 on v0

v1 whole, which is shorter than its diff:
```python
import functools

import jax
import jax.numpy as jnp
from jax import lax
from jax.experimental import pallas as pl
from jax.experimental.pallas import tpu as pltpu
from jax.sharding import PartitionSpec as P


LANES = 128
TAPS = 7
HEAD = TAPS - 1
SUB = 8
VMEM_LIMIT = 12 * 1024 * 1024


def specs(kinds):
    return [
        pl.BlockSpec(memory_space=pltpu.SMEM if k == "s" else pltpu.VMEM) for k in kinds
    ]


def doc_start(lengths, position):
    start, found = jnp.int32(0), jnp.zeros_like(position)
    for doc in range(lengths.shape[0]):
        found = jnp.where(position >= start, jnp.maximum(found, start), found)
        start = start + lengths[doc]
    return found


def short_conv(shifts, x, taps):
    tokens = x.shape[0]
    moved = jnp.dot(shifts, x, preferred_element_type=jnp.float32)
    total = x.astype(jnp.float32) * taps(0)
    for i in range(1, TAPS):
        total = total + moved[(i - 1) * tokens : i * tokens] * taps(i)
    return total.astype(jnp.bfloat16)


def rows_of(shape, dim=0):
    return lax.broadcasted_iota(jnp.int32, shape, dim)


def front_body(lengths, here, feats, taps, decay, msg, prod, shifts, stage):
    _, tokens, channels = feats.shape
    modes = decay.shape[0]
    groups = channels // LANES
    row = rows_of((tokens, tokens))
    column = rows_of((tokens, tokens), 1)
    position = row + here[0] * tokens
    reach = position - doc_start(lengths, position)
    for i in range(1, TAPS):
        hit = (column == row - i) & (reach >= i)
        shifts[(i - 1) * tokens : i * tokens, :] = jnp.where(hit, 1.0, 0.0).astype(jnp.bfloat16)
    states = groups * modes
    weights_row = rows_of((SUB, LANES)).astype(jnp.float32)
    wide = 2 * LANES
    for block in range(channels // wide):
        lanes = slice(block * wide, (block + 1) * wide)
        first, third = (
            short_conv(shifts[...], feats[b, :, lanes], lambda i, b=b: taps[b, i : i + 1, lanes])
            for b in (0, 2)
        )
        product = first.astype(jnp.float32) * third.astype(jnp.float32)
        product = jnp.where(rows_of((tokens, wide)) >= HEAD, product, 0.0).astype(jnp.bfloat16)
        prod[:, lanes] = product
        values = product.astype(jnp.float32)
        for half in range(wide // LANES):
            j = block * (wide // LANES) + half
            mine = slice(j * LANES, (j + 1) * LANES)
            v = values[:, half * LANES : (half + 1) * LANES]
            for m in range(modes):
                rate = decay[m : m + 1, mine]
                step = jnp.broadcast_to(jnp.exp(-SUB * rate), (SUB, LANES))
                state = v[0:SUB]
                for q in range(1, tokens // SUB):
                    state = state * step + v[q * SUB : (q + 1) * SUB]
                state = state * jnp.exp(-rate * (SUB - 1 - weights_row))
                end = jnp.sum(state, axis=0, keepdims=True)
                high = end.astype(jnp.bfloat16).astype(jnp.float32)
                stage[j * modes + m : j * modes + m + 1, :] = high
                stage[states + j * modes + m : states + j * modes + m + 1, :] = end - high
            at = 2 * states
            for b, low in ((0, tokens - HEAD), (2, tokens - HEAD), (1, tokens - HEAD), (0, 0), (2, 0)):
                part = feats[b, tokens - 2 * SUB : tokens, mine] if low else feats[b, 0 : 2 * SUB, mine]
                part = part.astype(jnp.float32)
                skip = 2 * SUB - HEAD if low else 0
                for r in range(HEAD):
                    stage[at + r * groups + j : at + r * groups + j + 1, :] = part[skip + r : skip + r + 1]
                at += HEAD * groups
    used = 2 * states + 5 * HEAD * groups
    if used < stage.shape[0]:
        stage[used:, :] = jnp.zeros((stage.shape[0] - used, LANES), jnp.float32)
    for c in range(stage.shape[0] // LANES):
        msg[:, c * LANES : (c + 1) * LANES] = stage[c * LANES : (c + 1) * LANES, :].T.astype(jnp.bfloat16)


def local_body(here, feats, taps, decay, residue, prod, shifts, gate, near, grow, rate_o, weight_o, taps_o, table):
    _, tokens, channels = feats.shape
    modes = decay.shape[0]
    groups = channels // LANES
    chunks = tokens // SUB
    wide = 2 * LANES
    for block in range(channels // wide):
        lanes = slice(block * wide, (block + 1) * wide)
        gate[:, lanes] = short_conv(shifts[...], feats[1, :, lanes], lambda i: taps[1, i : i + 1, lanes])
    owned = rows_of((modes, LANES), 1) == here[0]
    owned_taps = rows_of((TAPS, LANES), 1) == here[0]
    for j in range(groups):
        mine = slice(j * LANES, (j + 1) * LANES)
        at = slice(j * modes, (j + 1) * modes)
        rates, scale = decay[:, mine], residue[:, mine]
        scale = scale * jnp.sqrt(2.0 * rates)
        pick = jnp.sum(jnp.where(owned, rates, 0.0), axis=1, keepdims=True)
        rate_o[at, :] = jnp.broadcast_to(pick, (modes, LANES))
        pick = jnp.sum(jnp.where(owned, scale, 0.0), axis=1, keepdims=True)
        weight_o[at, :] = jnp.broadcast_to(pick, (modes, LANES))
        for b in range(3):
            pick = jnp.sum(jnp.where(owned_taps, taps[b, :, mine], 0.0), axis=1, keepdims=True)
            pick = jnp.broadcast_to(pick, (TAPS, LANES))
            for i in range(TAPS):
                to = (b * TAPS + i) * groups + j
                taps_o[to : to + 1, :] = pick[i : i + 1]
    inside = rows_of((SUB, LANES))
    steps = inside.astype(jnp.float32)

    def group(j, carry):
        mine = pl.ds(pl.multiple_of(j * LANES, LANES), LANES)
        sums = [jnp.zeros((SUB, LANES), jnp.float32) for _ in range(chunks)]
        for m in range(modes):
            rate = decay[m : m + 1, mine]
            weight = residue[m : m + 1, mine] * jnp.sqrt(2.0 * rate)
            step = jnp.broadcast_to(jnp.exp(-SUB * rate), (SUB, LANES))
            grow[m * SUB : (m + 1) * SUB, mine] = weight * jnp.exp(-rate * (steps + (SUB - HEAD + 1)))
            wave = weight * jnp.exp(-rate * steps)
            for q in range(chunks):
                sums[q] = sums[q] + wave
                if q + 1 < chunks:
                    wave = wave * step
        for q in range(chunks):
            table[q * SUB : (q + 1) * SUB, :] = sums[q]
        values = prod[:, mine].astype(jnp.float32)
        total = [jnp.zeros((SUB, LANES), jnp.float32) for _ in range(chunks)]
        for k in range(SUB):
            if k:
                turned = [
                    pltpu.roll(values[q * SUB : (q + 1) * SUB], k, 0) for q in range(chunks)
                ]
                low = inside < k
                moved = [
                    jnp.where(low, turned[q - 1] if q else 0.0, turned[q]) for q in range(chunks)
                ]
            else:
                moved = [values[q * SUB : (q + 1) * SUB] for q in range(chunks)]
            for d in range(chunks):
                factor = jnp.broadcast_to(table[d * SUB + k : d * SUB + k + 1, :], (SUB, LANES))
                for q in range(d, chunks):
                    total[q] = total[q] + factor * moved[q - d]
        for q in range(chunks):
            near[q * SUB : (q + 1) * SUB, mine] = total[q]
        return carry

    lax.fori_loop(0, groups, group, 0)


def owner_body(lengths, arrived, rate_o, weight_o, taps_o, back, stage, out, *, tokens):
    blocks = arrived.shape[0]
    states = rate_o.shape[0]
    groups = taps_o.shape[0] // (3 * TAPS)
    modes = states // groups
    for c in range(stage.shape[0] // LANES):
        stage[c * LANES : (c + 1) * LANES, :] = arrived[:, c * LANES : (c + 1) * LANES].astype(jnp.float32).T
    lane = rows_of((groups, blocks), 1)
    base = 2 * states

    def part(k, r):
        at = base + (k * HEAD + r) * groups
        return stage[at : at + groups, :]

    def before(k, r):
        return jnp.where(lane >= 1, pltpu.roll(part(k, r), 1, 1), 0.0)

    reach = []
    for r in range(HEAD):
        position = lane * tokens + r
        reach.append(position - doc_start(lengths, position))
    heads = []
    for last, first, b in ((0, 3, 0), (1, 4, 2)):
        ext = [before(last, r) for r in range(HEAD)] + [part(first, r) for r in range(HEAD)]
        found = []
        for r in range(HEAD):
            total = jnp.zeros((groups, blocks), jnp.float32)
            for i in range(TAPS):
                at = (b * TAPS + i) * groups
                term = taps_o[at : at + groups, :] * ext[HEAD + r - i]
                total = total + jnp.where(reach[r] >= i, term, 0.0)
            found.append(total.astype(jnp.bfloat16).astype(jnp.float32))
        heads.append(found)
    products = [(a * b).astype(jnp.bfloat16).astype(jnp.float32) for a, b in zip(*heads)]
    lane = rows_of((modes, blocks), 1)
    for j in range(groups):
        at = slice(j * modes, (j + 1) * modes)
        rate, weight = rate_o[at, :], weight_o[at, :]
        ratio = jnp.exp(-rate)
        rows = [jnp.broadcast_to(p[j : j + 1], (modes, blocks)) for p in products]
        head = rows[0]
        for r in range(1, HEAD):
            head = head * ratio + rows[r]
        total = stage[at, :] + stage[states + j * modes : states + (j + 1) * modes, :]
        total = total + jnp.exp(-rate * (tokens - HEAD)) * head
        distance = 1
        while distance < blocks:
            shifted = jnp.where(lane >= distance, pltpu.roll(total, distance, 1), 0.0)
            total = total + jnp.exp(-rate * float(tokens * distance)) * shifted
            distance *= 2
        state = jnp.where(lane >= 1, pltpu.roll(total, 1, 1), 0.0)
        for r in range(HEAD):
            state = state * ratio + rows[r]
            to = 2 * states + r * groups + j
            out[to : to + 1, :] = jnp.sum(state * weight, axis=0, keepdims=True)
        high = state.astype(jnp.bfloat16).astype(jnp.float32)
        out[at, :] = high
        out[states + j * modes : states + (j + 1) * modes, :] = state - high
    at = 2 * states + HEAD * groups
    for r in range(HEAD):
        out[at + r * groups : at + (r + 1) * groups, :] = before(2, r)
    used = 2 * states + 2 * HEAD * groups
    if used < out.shape[0]:
        out[used:, :] = jnp.zeros((out.shape[0] - used, LANES), jnp.float32)
    for c in range(out.shape[0] // LANES):
        back[:, c * LANES : (c + 1) * LANES] = out[c * LANES : (c + 1) * LANES, :].T.astype(jnp.bfloat16)


def join_body(lengths, here, back, near, gate, grow, decay, feats, taps, gated, energy, stage):
    tokens, channels = near.shape
    modes = decay.shape[0]
    groups = channels // LANES
    chunks = tokens // SUB
    states = groups * modes
    for c in range(stage.shape[0] // LANES):
        stage[c * LANES : (c + 1) * LANES, :] = back[:, c * LANES : (c + 1) * LANES].astype(jnp.float32).T
    inside = rows_of((SUB, LANES))
    position = inside + here[0] * tokens
    reach = position - doc_start(lengths, position)
    squares = [jnp.zeros((SUB, LANES), jnp.float32) for _ in range(chunks)]
    for j in range(groups):
        mine = slice(j * LANES, (j + 1) * LANES)
        total = [near[q * SUB : (q + 1) * SUB, mine] for q in range(chunks)]
        for m in range(modes):
            at = j * modes + m
            state = stage[at : at + 1, :] + stage[states + at : states + at + 1, :]
            rate = decay[m : m + 1, mine]
            step = jnp.broadcast_to(jnp.exp(-SUB * rate), (SUB, LANES))
            wave = grow[m * SUB : (m + 1) * SUB, mine] * state
            total[0] = total[0] + wave * jnp.exp(SUB * rate)
            for q in range(1, chunks):
                total[q] = total[q] + wave
                if q + 1 < chunks:
                    wave = wave * step
        at = 2 * states + j
        pieces = [stage[at + r * groups : at + r * groups + 1, :] for r in range(HEAD)]
        top = jnp.concatenate(pieces + [total[0][HEAD:SUB]], axis=0)
        total[0] = top
        at += HEAD * groups
        pieces = [stage[at + r * groups : at + r * groups + 1, :] for r in range(HEAD)]
        current = feats[1, 0 : 2 * SUB, mine].astype(jnp.float32)[0:SUB]
        ext = jnp.concatenate(pieces + [current, jnp.zeros((2, LANES), jnp.float32)], axis=0)
        front = jnp.zeros((SUB, LANES), jnp.float32)
        for i in range(TAPS):
            term = taps[1, i : i + 1, mine] * ext[HEAD - i : HEAD - i + SUB]
            front = front + jnp.where(reach >= i, term, 0.0)
        front = front.astype(jnp.bfloat16).astype(jnp.float32)
        gates = gate[:, mine].astype(jnp.float32)
        for q in range(chunks):
            g = gates[q * SUB : (q + 1) * SUB] if q else front
            value = g * total[q].astype(jnp.bfloat16).astype(jnp.float32)
            gated[q * SUB : (q + 1) * SUB, mine] = value
            squares[q] = squares[q] + value * value
    summed = jnp.sum(jnp.concatenate(squares, axis=0), axis=1, keepdims=True)
    energy[...] = jnp.broadcast_to(summed, (tokens, LANES)).T[0:1, :]


def scale_body(energy, gated, gain, mixed, *, width):
    tokens, channels = gated.shape
    scaling = lax.rsqrt(energy[...] / width + 1e-06)
    scaling = jnp.broadcast_to(scaling, (LANES, tokens)).T
    for j in range(channels // LANES):
        mine = slice(j * LANES, (j + 1) * LANES)
        mixed[:, mine] = (gated[:, mine] * scaling * gain[:, mine]).astype(jnp.bfloat16)


def exchange(block):
    blocks, width = block.shape
    moved = lax.all_to_all(
        block.reshape(blocks, 2, width // 2), ("gr", "gc"), split_axis=0, concat_axis=0, tiled=True
    )
    return moved.reshape(blocks, width)


def padded(rows):
    return -(-rows // (2 * LANES)) * 2 * LANES


def per_device(features, short_taps, decay, residue, doc_lengths, gain):
    _, tokens, channels = features.shape
    modes = decay.shape[0]
    blocks = lax.axis_size(("gr", "gc"))
    groups = channels // LANES
    states = groups * modes
    here = lax.axis_index(("gr", "gc")).astype(jnp.int32).reshape(1)
    f32, bf16 = jnp.float32, jnp.bfloat16
    sds = jax.ShapeDtypeStruct
    out_rows = padded(2 * states + 5 * HEAD * groups)
    msg, prod, shifts = pl.pallas_call(
        front_body,
        out_shape=(
            sds((blocks, out_rows), bf16),
            sds((tokens, channels), bf16),
            sds((HEAD * tokens, tokens), bf16),
        ),
        in_specs=specs("ssvvv"),
        out_specs=specs("vvv"),
        scratch_shapes=[pltpu.VMEM((out_rows, LANES), f32)],
        compiler_params=pltpu.CompilerParams(vmem_limit_bytes=VMEM_LIMIT),
        cost_estimate=pl.CostEstimate(flops=10**7, bytes_accessed=4 * 10**6, transcendentals=0),
        name="front",
    )(doc_lengths, here, features, short_taps, decay)
    arrived = exchange(msg)
    gate, near, grow, rate_o, weight_o, taps_o = pl.pallas_call(
        local_body,
        out_shape=(
            sds((tokens, channels), bf16),
            sds((tokens, channels), f32),
            sds((modes * SUB, channels), f32),
            sds((states, LANES), f32),
            sds((states, LANES), f32),
            sds((3 * TAPS * groups, LANES), f32),
        ),
        in_specs=specs("svvvvvv"),
        out_specs=specs("vvvvvv"),
        scratch_shapes=[pltpu.VMEM((tokens, LANES), f32)],
        compiler_params=pltpu.CompilerParams(vmem_limit_bytes=VMEM_LIMIT),
        cost_estimate=pl.CostEstimate(flops=10**8, bytes_accessed=8 * 10**6, transcendentals=0),
        name="local",
    )(here, features, short_taps, decay, residue, prod, shifts)
    back_rows = padded(2 * states + 2 * HEAD * groups)
    back = pl.pallas_call(
        functools.partial(owner_body, tokens=tokens),
        out_shape=sds((blocks, back_rows), bf16),
        in_specs=specs("svvvv"),
        out_specs=specs("v")[0],
        scratch_shapes=[pltpu.VMEM((out_rows, LANES), f32), pltpu.VMEM((back_rows, LANES), f32)],
        compiler_params=pltpu.CompilerParams(vmem_limit_bytes=VMEM_LIMIT),
        cost_estimate=pl.CostEstimate(flops=10**6, bytes_accessed=10**6, transcendentals=0),
        name="owner",
    )(doc_lengths, arrived, rate_o, weight_o, taps_o)
    given = exchange(back)
    gated, energy = pl.pallas_call(
        join_body,
        out_shape=(sds((tokens, channels), f32), sds((1, tokens), f32)),
        in_specs=specs("ssvvvvvvv"),
        out_specs=specs("vv"),
        scratch_shapes=[pltpu.VMEM((back_rows, LANES), f32)],
        compiler_params=pltpu.CompilerParams(vmem_limit_bytes=VMEM_LIMIT),
        cost_estimate=pl.CostEstimate(flops=10**7, bytes_accessed=5 * 10**6, transcendentals=0),
        name="join",
    )(doc_lengths, here, given, near, gate, grow, decay, features, short_taps)
    energy = lax.psum(energy, "ch")
    width = float(channels * lax.axis_size("ch"))
    return pl.pallas_call(
        functools.partial(scale_body, width=width),
        out_shape=sds((tokens, channels), bf16),
        in_specs=specs("vvv"),
        out_specs=specs("v")[0],
        compiler_params=pltpu.CompilerParams(vmem_limit_bytes=VMEM_LIMIT),
        cost_estimate=pl.CostEstimate(flops=10**6, bytes_accessed=2 * 10**6, transcendentals=0),
        name="scale",
    )(energy, gated, gain.reshape(1, channels))


def solution(mesh):
    placed = (
        P(None, ("gr", "gc"), "ch"),
        P(None, None, "ch"),
        P(None, "ch"),
        P(None, "ch"),
        P(),
        P("ch"),
    )
    return jax.shard_map(
        per_device, mesh=mesh, in_specs=placed, out_specs=P(("gr", "gc"), "ch"), check_vma=False
    )
```

time: 592 us -> 109 us (0.18)
  the two profiles are of different devices: /device:TPU:32 before, /device:TPU:2 now
where the time goes in v1:
time: 109 us
  blocking collectives  46.5 us (43%)
  starting transfers between devices  20 us (18%)
  local copies, waits for them, and re-layouts  18.7 us (17%)
  Pallas kernels  17.7 us (16%)
  waiting for transfers between devices  5.65 us (5%)
    all_to_all x1, blocking collectives, exchange(): lax.all_to_all(block.reshape(blocks, 2, width // 2), ('gr', 'gc'), split_...  27.6 us
    all_to_all x1, starting transfers between devices, exchange(): lax.all_to_all(block.reshape(blocks, 2, width // 2), ('gr', 'gc'), split_...  20 us
    psum x1, blocking collectives, per_device(): energy = lax.psum(energy, 'ch')  18.9 us
    unnamed x50, local copies, waits for them, and re-layouts  17.8 us
    pallas_call x1, Pallas kernels, per_device(): pl.pallas_call(local_body, out_shape=(sds((tokens, channels), bf16), sds(...  7.96 us
    all_to_all x1, waiting for transfers between devices, exchange(): lax.all_to_all(block.reshape(blocks, 2, width // 2), ('gr', 'gc'), split_...  5.65 us
    pallas_call x1, Pallas kernels, per_device(): pl.pallas_call(front_body, out_shape=(sds((blocks, out_rows), bf16), sds(...  4.09 us
    pallas_call x1, Pallas kernels, per_device(): pl.pallas_call(join_body, out_shape=(sds((tokens, channels), f32), sds((1...  2.97 us
  transfers between devices with their start and end apart: 1, of which 1 were waited for; matrix products, arithmetic and copies ran while one was open for 0% of the time, Pallas kernels for 7%

profile of v1, /device:TPU:2, one launch (start us, length us, event | category | flops | bytes accessed | tf_op | source)
XLA Modules:
  0.0 108.7 jit_solution(9158053188336033796)
XLA Ops:
  0.0 0.0 copy-start
  0.0 1.4 %copy-done = bf16[3,128,2048]{2,1,0:T(8,128)(2,1)S(1)} copy-done((bf16[3,128,2048]{2,1,0:T(8,128)(2,1)S(1)}, bf16[3,128,2048]{2,1,0:T(8,128)(2,1)}, u32[]{:S(2)}) %copy-start) | copy-done | bytes 1572888
  1.4 0.0 copy-start.2
  1.4 0.9 copy-done.2
  2.3 0.0 copy-start.4
  2.3 0.9 copy-done.4
  3.2 0.0 copy-start.22
  3.2 0.7 copy-done.22
  3.9 0.0 copy-start.1
  3.9 0.0 copy-start.3
  3.9 0.0 copy-start.5
  3.9 4.1 %front.1 = (bf16[128,1024]{1,0:T(8,128)(2,1)S(1)}, bf16[128,2048]{1,0:T(8,128)(2,1)S(1)}, bf16[768,128]{1,0:T(8,128)(2,1)S(1)}) custom-call(s32[8]{0:T(128)S(1)} %copy-done.22, s32[1]{0:T(128)} %bitcast.here, bf16[3,128,2048]{2,1,0:T(8,128)(2,1)S(1)} %copy-done, f32[3,7,2048]{2,1,0:T(8,128)S(1)} %copy-done.2, f32[16,2048]{1,0:T(8,128)S(1)} %copy-done.4), custom_call_target="tpu_custom_call" | custom-call | flops 10000000 | bytes 4000000 | tf_op jit(solution)/shard_map/front/pallas_call | solution.py:315
  8.0 0.0 copy-start.12
  8.0 0.9 reshape.19
  8.9 20.0 %all-to-all-start = ((bf16[128,2,512]{2,1,0:T(2,128)(2,1)}), bf16[128,2,512]{2,1,0:T(2,128)(2,1)}, u32[]{:S(2)}, u32[]{:S(2)}) async-start(bf16[128,2,512]{2,1,0:T(2,128)(2,1)} %reshape.19), calls=%async_computation | async-start | bytes 524288 | tf_op jit(solution)/shard_map/all_to_all | solution.py:295
  29.0 0.0 copy-done.12
  29.0 0.0 copy-done.1
  29.0 0.0 copy-done.3
  29.0 0.0 copy-done.5
  29.0 0.0 copy-start.13
  29.0 0.9 copy-done.13
  29.9 0.9 copy-done.16
  30.8 8.0 %local.1 = (bf16[128,2048]{1,0:T(8,128)(2,1)S(1)}, f32[128,2048]{1,0:T(8,128)S(1)}, f32[128,2048]{1,0:T(8,128)S(1)}, f32[256,128]{1,0:T(8,128)S(1)}, f32[256,128]{1,0:T(8,128)S(1)}, /*index=5*/f32[336,128]{1,0:T(8,128)S(1)}) custom-call(s32[1]{0:T(128)} %bitcast.here, bf16[3,128,2048]{2,1,0:T(8,128)(2,1)S(1)} %copy-done.1, f32[3,7,2048]{2,1,0:T(8,128)S(1)} %copy-done.3, ...), custom_call_target="tpu_custom_call" | custom-call | flops 100000000 | bytes 8000000 | tf_op jit(solution)/shard_map/local/pallas_call | solution.py:330
  38.8 0.0 copy-start.6
  38.8 1.0 copy-done.6
  39.8 0.8 copy-done.10
  40.6 0.7 copy-done.14
  41.3 0.6 copy-done.17
  41.9 0.6 copy-done.19
  42.6 5.7 %all-to-all-done = bf16[128,2,512]{2,1,0:T(2,128)(2,1)} async-done(((bf16[128,2,512]{2,1,0:T(2,128)(2,1)}), bf16[128,2,512]{2,1,0:T(2,128)(2,1)}, u32[]{:S(2)}, u32[]{:S(2)}) %all-to-all-start) | async-done | bytes 262176 | tf_op jit(solution)/shard_map/all_to_all | solution.py:295
  48.2 1.0 copy.7
  49.2 0.0 copy-done.23
  49.2 0.0 copy-start.15
  49.2 0.9 copy-done.15
  50.1 0.9 copy-done.18
  51.1 0.9 copy-done.20
  52.0 1.7 %owner.1 = bf16[128,768]{1,0:T(8,128)(2,1)S(1)} custom-call(s32[8]{0:T(128)S(1)} %copy-done.23, bf16[128,1024]{1,0:T(8,128)(2,1)S(1)} %bitcast.6, f32[256,128]{1,0:T(8,128)S(1)} %copy-done.18, f32[256,128]{1,0:T(8,128)S(1)} %copy-done.20, f32[336,128]{1,0:T(8,128)S(1)} %copy-done.15), custom_call_target="tpu_custom_call" | custom-call | flops 1000000 | bytes 1000000 | tf_op jit(solution)/shard_map/owner/pallas_call | solution.py:348
  53.6 0.1 reshape.21
  53.7 27.6 %all_to_all.10 = bf16[128,2,384]{2,1,0:T(2,128)(2,1)S(1)} all-to-all(bf16[128,2,384]{2,1,0:T(2,128)(2,1)S(1)} %reshape.21), channel_id=1, replica_groups=mesh['ch'=4,'gr'=16,'gc'=8] {'gr','gc'}, dimensions={0} | all-to-all | bytes 393216 | tf_op jit(solution)/shard_map/all_to_all | solution.py:295
  81.3 0.0 copy-start.7
  81.3 1.2 %copy-done.7 = f32[128,2048]{1,0:T(8,128)S(1)} copy-done((f32[128,2048]{1,0:T(8,128)S(1)}, f32[128,2048]{1,0:T(8,128)}, u32[]{:S(2)}) %copy-start.7) | copy-done | bytes 1048600
  82.5 1.0 copy-done.11
  83.6 3.0 %join.1 = (f32[128,2048]{1,0:T(8,128)S(1)}, f32[1,128]{1,0:T(1,128)S(1)}) custom-call(s32[8]{0:T(128)S(1)} %copy-done.23, s32[1]{0:T(128)} %bitcast.here, bf16[128,768]{1,0:T(8,128)(2,1)S(1)} %bitcast.7, f32[128,2048]{1,0:T(8,128)S(1)} %get-tuple-element.22.near, bf16[128,2048]{1,0:T(8,128)(2,1)S(1)} %copy-done.11, f32[128,2048]{1,0:T(8,128)S(1)} %copy-done.7, ...), custom_call_target="tpu_custom_call" | custom-call | flops 10000000 | bytes 5000000 | tf_op jit(solution)/shard_map/join/pallas_call | solution.py:359
  86.5 1.1 copy-done.8
  87.6 18.9 %psum.7.energy = f32[1,128]{1,0:T(1,128)S(1)} all-reduce(f32[1,128]{1,0:T(1,128)S(1)} %get-tuple-element.25), channel_id=1, replica_groups=mesh['ch'=4,'gr'=16,'gc'=8] {'ch'}, use_global_device_ids=true, to_apply=%region_0.0 | all-reduce | flops 128 | bytes 1024 | tf_op jit(solution)/shard_map/psum | solution.py:369
  106.5 0.0 copy-done.21
  106.5 1.2 %copy-done.9 = f32[128,2048]{1,0:T(8,128)S(1)} copy-done((f32[128,2048]{1,0:T(8,128)S(1)}, f32[128,2048]{1,0:T(8,128)}, u32[]{:S(2)}) %copy-start.9) | copy-done | bytes 1048600
  107.8 1.0 scale.1
  (13 shorter events, 0.0 us)
Async XLA Ops:
  0.0 1.4 %copy-start = (bf16[3,128,2048]{2,1,0:T(8,128)(2,1)S(1)}, bf16[3,128,2048]{2,1,0:T(8,128)(2,1)}, u32[]{:S(2)}) copy-start(bf16[3,128,2048]{2,1,0:T(8,128)(2,1)} %feats.5) | copy-start | bytes 4718596
  1.4 0.9 copy-start.2
  2.3 0.9 copy-start.4
  3.2 0.7 copy-start.22
  3.9 25.1 %copy-start.1 = (bf16[3,128,2048]{2,1,0:T(8,128)(2,1)S(1)}, bf16[3,128,2048]{2,1,0:T(8,128)(2,1)}, u32[]{:S(2)}) copy-start(bf16[3,128,2048]{2,1,0:T(8,128)(2,1)} %feats.5) | copy-start | bytes 4718596
  3.9 25.1 %copy-start.3 = (f32[3,7,2048]{2,1,0:T(8,128)S(1)}, f32[3,7,2048]{2,1,0:T(8,128)}, u32[]{:S(2)}) copy-start(f32[3,7,2048]{2,1,0:T(8,128)} %taps.5) | copy-start | bytes 516100
  3.9 25.1 %copy-start.5 = (f32[16,2048]{1,0:T(8,128)S(1)}, f32[16,2048]{1,0:T(8,128)}, u32[]{:S(2)}) copy-start(f32[16,2048]{1,0:T(8,128)} %decay.5) | copy-start | bytes 393220
  8.0 21.0 %copy-start.12 = (bf16[768,128]{1,0:T(8,128)(2,1)}, bf16[768,128]{1,0:T(8,128)(2,1)S(1)}, u32[]{:S(2)}) copy-start(bf16[768,128]{1,0:T(8,128)(2,1)S(1)} %get-tuple-element.18.shifts) | copy-start | bytes 589828
  8.9 39.3 %all-to-all-start = ((bf16[128,2,512]{2,1,0:T(2,128)(2,1)}), bf16[128,2,512]{2,1,0:T(2,128)(2,1)}, u32[]{:S(2)}, u32[]{:S(2)}) async-start(bf16[128,2,512]{2,1,0:T(2,128)(2,1)} %reshape.19), calls=%async_computation | async-start | bytes 524288 | tf_op jit(solution)/shard_map/all_to_all | solution.py:295
  29.0 0.9 copy-start.13
  29.9 0.9 copy-start.16
  30.8 18.4 %copy-start.23 = (s32[8]{0:T(128)S(1)}, s32[8]{0:T(128)}, u32[]{:S(2)}) copy-start(s32[8]{0:T(128)} %lengths.5) | copy-start | bytes 100
  38.8 1.0 copy-start.6
  39.8 0.8 copy-start.10
  40.6 0.7 copy-start.14
  41.3 0.7 copy-start.17
  41.9 0.6 copy-start.19
  49.2 0.9 copy-start.15
  50.1 0.9 copy-start.18
  51.0 0.9 copy-start.20
  81.3 1.2 %copy-start.7 = (f32[128,2048]{1,0:T(8,128)S(1)}, f32[128,2048]{1,0:T(8,128)}, u32[]{:S(2)}) copy-start(f32[128,2048]{1,0:T(8,128)} %copy-done.6) | copy-start | bytes 3145732
  82.5 1.0 copy-start.11
  83.5 23.0 %copy-start.21 = (f32[2048]{0:T(1024)S(1)}, f32[2048]{0:T(1024)}, u32[]{:S(2)}) copy-start(f32[2048]{0:T(1024)} %param.11) | copy-start | bytes 24580
  86.5 1.1 copy-start.8
  106.5 1.2 %copy-start.9 = (f32[128,2048]{1,0:T(8,128)S(1)}, f32[128,2048]{1,0:T(8,128)}, u32[]{:S(2)}) copy-start(f32[128,2048]{1,0:T(8,128)} %copy-done.8) | copy-start | bytes 3145732

commit v2 on v1

v2 whole, which is shorter than its diff:
```python
import functools

import jax
import jax.numpy as jnp
from jax import lax
from jax.experimental import pallas as pl
from jax.experimental.pallas import tpu as pltpu
from jax.sharding import PartitionSpec as P


LANES = 128
TAPS = 7
HEAD = TAPS - 1
SUB = 8
VMEM_LIMIT = 12 * 1024 * 1024


def doc_start(lengths, position):
    start, found = jnp.int32(0), jnp.zeros_like(position)
    for doc in range(lengths.shape[0]):
        found = jnp.where(position >= start, jnp.maximum(found, start), found)
        start = start + lengths[doc]
    return found


def short_conv(shifts, x, taps):
    tokens = x.shape[0]
    moved = jnp.dot(shifts, x, preferred_element_type=jnp.float32)
    total = x.astype(jnp.float32) * taps(0)
    for i in range(1, TAPS):
        total = total + moved[(i - 1) * tokens : i * tokens] * taps(i)
    return total.astype(jnp.bfloat16)


def rows_of(shape, dim=0):
    return lax.broadcasted_iota(jnp.int32, shape, dim)


def powers(ratio):
    square = ratio * ratio
    fourth = square * square
    return ratio, square, fourth, fourth * fourth


def spread(row, rows=SUB):
    return jnp.broadcast_to(row, (rows, row.shape[1]))


def fill_shifts(shifts, lengths, first_token):
    tokens = shifts.shape[1]
    row = rows_of((tokens, tokens))
    column = rows_of((tokens, tokens), 1)
    position = row + first_token
    reach = position - doc_start(lengths, position)
    for i in range(1, TAPS):
        hit = (column == row - i) & (reach >= i)
        shifts[(i - 1) * tokens : i * tokens, :] = jnp.where(hit, 1.0, 0.0).astype(jnp.bfloat16)


def front_body(
    lengths_hbm, here, feats_hbm, taps_hbm, decay_hbm, msg, prod_hbm, stage, feats, taps, decay, prod, shifts, lengths, sems
):
    _, tokens, channels = feats.shape
    modes = decay.shape[0]
    groups = channels // LANES
    wide = 2 * LANES
    count = channels // wide

    def fetched(block):
        lanes = slice(block * wide, (block + 1) * wide)
        return pltpu.make_async_copy(feats_hbm.at[:, :, lanes], feats.at[:, :, lanes], sems.at[3 + block])

    def stored(block):
        lanes = slice(block * wide, (block + 1) * wide)
        return pltpu.make_async_copy(prod.at[:, lanes], prod_hbm.at[:, lanes], sems.at[3 + count + block])

    counted = pltpu.make_async_copy(lengths_hbm, lengths, sems.at[0])
    others = (
        pltpu.make_async_copy(taps_hbm, taps, sems.at[1]),
        pltpu.make_async_copy(decay_hbm, decay, sems.at[2]),
    )
    counted.start()
    fetched(0).start()
    for copy in others:
        copy.start()
    for block in range(1, count):
        fetched(block).start()
    states = groups * modes
    used = states + 5 * HEAD * groups
    if used < stage.shape[0]:
        stage[used:, :] = jnp.zeros((stage.shape[0] - used, LANES), jnp.float32)
    counted.wait()
    fill_shifts(shifts, lengths, here[0] * tokens)
    for copy in others:
        copy.wait()
    for block in range(count):
        lanes = slice(block * wide, (block + 1) * wide)
        fetched(block).wait()
        first, third = (
            short_conv(shifts[...], feats[b, :, lanes], lambda i, b=b: taps[b, i : i + 1, lanes])
            for b in (0, 2)
        )
        product = first.astype(jnp.float32) * third.astype(jnp.float32)
        product = jnp.where(rows_of((tokens, wide)) >= HEAD, product, 0.0).astype(jnp.bfloat16)
        prod[:, lanes] = product
        stored(block).start()
        values = product.astype(jnp.float32)
        for half in range(wide // LANES):
            j = block * (wide // LANES) + half
            mine = slice(j * LANES, (j + 1) * LANES)
            v = values[:, half * LANES : (half + 1) * LANES]
            tables = powers(jnp.exp(-decay[:, mine]))
            for m in range(modes):
                one, two, four, eight = (spread(t[m : m + 1]) for t in tables)
                state = v[0:SUB]
                for q in range(1, tokens // SUB):
                    state = state * eight + v[q * SUB : (q + 1) * SUB]
                state = state * four + pltpu.roll(state, SUB - 4, 0)
                state = state * two + pltpu.roll(state, SUB - 2, 0)
                state = state * one + pltpu.roll(state, SUB - 1, 0)
                stage[j * modes + m : j * modes + m + 1, :] = state[0:1]
            at = states
            for b, low in ((0, True), (2, True), (1, True), (0, False), (2, False)):
                part = feats[b, tokens - 2 * SUB : tokens, mine] if low else feats[b, 0 : 2 * SUB, mine]
                part = part.astype(jnp.float32)
                skip = 2 * SUB - HEAD if low else 0
                for r in range(HEAD):
                    stage[at + r * groups + j : at + r * groups + j + 1, :] = part[skip + r : skip + r + 1]
                at += HEAD * groups
    for c in range(stage.shape[0] // LANES):
        msg[:, c * LANES : (c + 1) * LANES] = stage[c * LANES : (c + 1) * LANES, :].T.astype(jnp.bfloat16)
    for block in range(count):
        stored(block).wait()


def local_body(
    lengths, here, feats_hbm, prod_hbm, taps, decay, residue, gate, near, edge, owned, table, feats, prod, shifts, sems
):
    tokens, channels = feats.shape
    modes = decay.shape[0]
    copies = (
        pltpu.make_async_copy(feats_hbm.at[1], feats, sems.at[0]),
        pltpu.make_async_copy(prod_hbm, prod, sems.at[1]),
    )
    for copy in copies:
        copy.start()
    fill_shifts(shifts, lengths, here[0] * tokens)
    for copy in copies:
        copy.wait()
    groups = channels // LANES
    chunks = tokens // SUB
    wide = 2 * LANES
    for block in range(channels // wide):
        lanes = slice(block * wide, (block + 1) * wide)
        gate[:, lanes] = short_conv(shifts[...], feats[:, lanes], lambda i: taps[1, i : i + 1, lanes])
    states = groups * modes
    edge[...] = feats[0 : 2 * SUB, :].astype(jnp.float32)[0:SUB]
    chosen = rows_of((modes, LANES), 1) == here[0]
    chosen_taps = rows_of((TAPS, LANES), 1) == here[0]
    for j in range(groups):
        mine = slice(j * LANES, (j + 1) * LANES)
        at = slice(j * modes, (j + 1) * modes)
        rates, scale = decay[:, mine], residue[:, mine]
        scale = scale * jnp.sqrt(2.0 * rates)
        pick = jnp.sum(jnp.where(chosen, rates, 0.0), axis=1, keepdims=True)
        owned[at, :] = jnp.broadcast_to(pick, (modes, LANES))
        pick = jnp.sum(jnp.where(chosen, scale, 0.0), axis=1, keepdims=True)
        owned[states + j * modes : states + (j + 1) * modes, :] = jnp.broadcast_to(pick, (modes, LANES))
        for b in range(3):
            pick = jnp.sum(jnp.where(chosen_taps, taps[b, :, mine], 0.0), axis=1, keepdims=True)
            pick = jnp.broadcast_to(pick, (TAPS, LANES))
            for i in range(TAPS):
                to = 2 * states + (b * TAPS + i) * groups + j
                owned[to : to + 1, :] = pick[i : i + 1]
    inside = rows_of((SUB, LANES))
    steps = inside.astype(jnp.float32)

    def group(j, carry):
        mine = pl.ds(pl.multiple_of(j * LANES, LANES), LANES)
        sums = [jnp.zeros((SUB, LANES), jnp.float32) for _ in range(chunks)]
        for m in range(modes):
            rate = decay[m : m + 1, mine]
            weight = residue[m : m + 1, mine] * jnp.sqrt(2.0 * rate)
            step = jnp.broadcast_to(jnp.exp(-SUB * rate), (SUB, LANES))
            wave = weight * jnp.exp(-rate * steps)
            for q in range(chunks):
                sums[q] = sums[q] + wave
                if q + 1 < chunks:
                    wave = wave * step
        for q in range(chunks):
            table[q * SUB : (q + 1) * SUB, :] = sums[q]
        values = prod[:, mine].astype(jnp.float32)
        total = [jnp.zeros((SUB, LANES), jnp.float32) for _ in range(chunks)]
        for k in range(SUB):
            if k:
                turned = [
                    pltpu.roll(values[q * SUB : (q + 1) * SUB], k, 0) for q in range(chunks)
                ]
                low = inside < k
                moved = [
                    jnp.where(low, turned[q - 1] if q else 0.0, turned[q]) for q in range(chunks)
                ]
            else:
                moved = [values[q * SUB : (q + 1) * SUB] for q in range(chunks)]
            for d in range(chunks):
                factor = jnp.broadcast_to(table[d * SUB + k : d * SUB + k + 1, :], (SUB, LANES))
                for q in range(d, chunks):
                    total[q] = total[q] + factor * moved[q - d]
        for q in range(chunks):
            near[q * SUB : (q + 1) * SUB, mine] = total[q]
        return carry

    lax.fori_loop(0, groups, group, 0)


def owner_body(lengths, arrived, owned, back, stage, out, *, tokens, modes):
    blocks = arrived.shape[0]
    groups = owned.shape[0] // (2 * modes + 3 * TAPS)
    states = modes * groups
    for c in range(stage.shape[0] // LANES):
        stage[c * LANES : (c + 1) * LANES, :] = arrived[:, c * LANES : (c + 1) * LANES].astype(jnp.float32).T
    lane = rows_of((groups, blocks), 1)

    def part(k, r):
        at = states + (k * HEAD + r) * groups
        return stage[at : at + groups, :]

    def before(k, r):
        return jnp.where(lane >= 1, pltpu.roll(part(k, r), 1, 1), 0.0)

    reach = []
    for r in range(HEAD):
        position = lane * tokens + r
        reach.append(position - doc_start(lengths, position))
    heads = []
    for last, first, b in ((0, 3, 0), (1, 4, 2)):
        ext = [before(last, r) for r in range(HEAD)] + [part(first, r) for r in range(HEAD)]
        found = []
        for r in range(HEAD):
            total = jnp.zeros((groups, blocks), jnp.float32)
            for i in range(TAPS):
                at = 2 * states + (b * TAPS + i) * groups
                term = owned[at : at + groups, :] * ext[HEAD + r - i]
                total = total + jnp.where(reach[r] >= i, term, 0.0)
            found.append(total.astype(jnp.bfloat16).astype(jnp.float32))
        heads.append(found)
    products = [(a * b).astype(jnp.bfloat16).astype(jnp.float32) for a, b in zip(*heads)]
    lane = rows_of((modes, blocks), 1)
    for j in range(groups):
        at = slice(j * modes, (j + 1) * modes)
        rate, weight = owned[at, :], owned[states + j * modes : states + (j + 1) * modes, :]
        ratio = jnp.exp(-rate)
        rows = [spread(p[j : j + 1], modes) for p in products]
        head = rows[0]
        for r in range(1, HEAD):
            head = head * ratio + rows[r]
        total = stage[at, :] + jnp.exp(-rate * (tokens - HEAD)) * head
        decline = jnp.exp(-rate * tokens)
        distance = 1
        while distance < blocks:
            shifted = jnp.where(lane >= distance, pltpu.roll(total, distance, 1), 0.0)
            total = total + decline * shifted
            decline = decline * decline
            distance *= 2
        state = jnp.where(lane >= 1, pltpu.roll(total, 1, 1), 0.0)
        for r in range(HEAD):
            state = state * ratio + rows[r]
            to = states + r * groups + j
            out[to : to + 1, :] = jnp.sum(state * weight, axis=0, keepdims=True)
        out[at, :] = state
    at = states + HEAD * groups
    for r in range(HEAD):
        out[at + r * groups : at + (r + 1) * groups, :] = before(2, r)
    used = states + 2 * HEAD * groups
    if used < out.shape[0]:
        out[used:, :] = jnp.zeros((out.shape[0] - used, LANES), jnp.float32)
    for c in range(out.shape[0] // LANES):
        back[:, c * LANES : (c + 1) * LANES] = out[c * LANES : (c + 1) * LANES, :].T.astype(jnp.bfloat16)


def join_body(lengths, here, back, near, gate, edge, decay, residue, taps, gated, energy, stage):
    tokens, channels = near.shape
    modes = decay.shape[0]
    groups = channels // LANES
    chunks = tokens // SUB
    states = groups * modes
    for c in range(stage.shape[0] // LANES):
        stage[c * LANES : (c + 1) * LANES, :] = back[:, c * LANES : (c + 1) * LANES].astype(jnp.float32).T
    inside = rows_of((SUB, LANES))
    position = inside + here[0] * tokens
    reach = position - doc_start(lengths, position)
    odd, pair, quad = ((inside & bit) != 0 for bit in (1, 2, 4))
    squares = [jnp.zeros((SUB, LANES), jnp.float32) for _ in range(chunks)]
    for j in range(groups):
        mine = slice(j * LANES, (j + 1) * LANES)
        total = [near[q * SUB : (q + 1) * SUB, mine] for q in range(chunks)]
        rates = decay[:, mine]
        tables = powers(jnp.exp(-rates))
        start = stage[j * modes : (j + 1) * modes, :] * residue[:, mine] * jnp.sqrt(2.0 * rates)
        start = start * tables[0] * tables[1]
        grown = jnp.exp(SUB * rates)
        for m in range(modes):
            one, two, four, eight = (spread(t[m : m + 1]) for t in tables)
            wave = spread(start[m : m + 1])
            wave = jnp.where(odd, wave * one, wave)
            wave = jnp.where(pair, wave * two, wave)
            wave = jnp.where(quad, wave * four, wave)
            total[0] = total[0] + wave * spread(grown[m : m + 1])
            for q in range(1, chunks):
                total[q] = total[q] + wave
                if q + 1 < chunks:
                    wave = wave * eight
        at = states + j
        pieces = [stage[at + r * groups : at + r * groups + 1, :] for r in range(HEAD)]
        total[0] = jnp.concatenate(pieces + [total[0][HEAD:SUB]], axis=0)
        at += HEAD * groups
        pieces = [stage[at + r * groups : at + r * groups + 1, :] for r in range(HEAD)]
        ext = jnp.concatenate(pieces + [edge[:, mine], jnp.zeros((2, LANES), jnp.float32)], axis=0)
        front = jnp.zeros((SUB, LANES), jnp.float32)
        for i in range(TAPS):
            term = taps[1, i : i + 1, mine] * ext[HEAD - i : HEAD - i + SUB]
            front = front + jnp.where(reach >= i, term, 0.0)
        front = front.astype(jnp.bfloat16).astype(jnp.float32)
        gates = gate[:, mine].astype(jnp.float32)
        for q in range(chunks):
            g = gates[q * SUB : (q + 1) * SUB] if q else front
            value = g * total[q].astype(jnp.bfloat16).astype(jnp.float32)
            gated[q * SUB : (q + 1) * SUB, mine] = value
            squares[q] = squares[q] + value * value
    summed = jnp.sum(jnp.concatenate(squares, axis=0), axis=1, keepdims=True)
    row = jnp.broadcast_to(summed, (tokens, LANES)).T[0:1, :]
    for k in range(energy.shape[0]):
        energy[k : k + 1, :] = row


def scale_body(energy, gated, gain, mixed, *, width):
    tokens, channels = gated.shape
    scaling = lax.rsqrt(jnp.sum(energy[...], axis=0, keepdims=True) / width + 1e-06)
    scaling = jnp.broadcast_to(scaling, (LANES, tokens)).T
    for j in range(channels // LANES):
        mine = slice(j * LANES, (j + 1) * LANES)
        mixed[:, mine] = (gated[:, mine] * scaling * gain[:, mine]).astype(jnp.bfloat16)


def exchange(block):
    blocks, width = block.shape
    moved = lax.all_to_all(
        block.reshape(blocks, 2, width // 2), ("gr", "gc"), split_axis=0, concat_axis=0, tiled=True
    )
    return moved.reshape(blocks, width)


def padded(rows):
    return -(-rows // (2 * LANES)) * 2 * LANES


def kernel(body, name, kinds, outs, scratch, flops, moved, given="vvvv"):
    spaces = {"s": pltpu.SMEM, "v": pltpu.VMEM, "h": pltpu.HBM}
    return pl.pallas_call(
        body,
        out_shape=outs,
        in_specs=[pl.BlockSpec(memory_space=spaces[k]) for k in kinds],
        out_specs=tuple(pl.BlockSpec(memory_space=spaces[k]) for k, _ in zip(given, outs)),
        scratch_shapes=scratch,
        compiler_params=pltpu.CompilerParams(vmem_limit_bytes=VMEM_LIMIT),
        cost_estimate=pl.CostEstimate(flops=flops, bytes_accessed=moved, transcendentals=0),
        name=name,
    )


def per_device(features, short_taps, decay, residue, doc_lengths, gain):
    _, tokens, channels = features.shape
    modes = decay.shape[0]
    blocks = lax.axis_size(("gr", "gc"))
    groups = channels // LANES
    states = groups * modes
    here = lax.axis_index(("gr", "gc")).astype(jnp.int32).reshape(1)
    f32, bf16 = jnp.float32, jnp.bfloat16
    sds = jax.ShapeDtypeStruct
    vmem = pltpu.VMEM
    out_rows = padded(states + 5 * HEAD * groups)
    back_rows = padded(states + 2 * HEAD * groups)
    front = kernel(
        front_body,
        "front",
        "hshhh",
        (sds((blocks, out_rows), bf16), sds((tokens, channels), bf16)),
        [
            vmem((out_rows, LANES), f32),
            vmem(features.shape, bf16),
            vmem(short_taps.shape, f32),
            vmem(decay.shape, f32),
            vmem((tokens, channels), bf16),
            vmem((HEAD * tokens, tokens), bf16),
            pltpu.SMEM(doc_lengths.shape, jnp.int32),
            pltpu.SemaphoreType.DMA((3 + 2 * (channels // (2 * LANES)),)),
        ],
        10**7,
        4 * 10**6,
        "vh",
    )
    far = functools.partial(pltpu.with_memory_space_constraint, memory_space=pltpu.HBM)
    msg, prod = front(far(doc_lengths), here, far(features), far(short_taps), far(decay))
    arrived = exchange(msg)
    local = kernel(
        local_body,
        "local",
        "sshhvvv",
        (
            sds((tokens, channels), bf16),
            sds((tokens, channels), f32),
            sds((SUB, channels), f32),
            sds((2 * states + 3 * TAPS * groups, LANES), f32),
        ),
        [
            vmem((tokens, LANES), f32),
            vmem((tokens, channels), bf16),
            vmem((tokens, channels), bf16),
            vmem((HEAD * tokens, tokens), bf16),
            pltpu.SemaphoreType.DMA((2,)),
        ],
        10**8,
        8 * 10**6,
    )
    gate, near, edge, owned = local(doc_lengths, here, far(features), far(prod), short_taps, decay, residue)
    owner = kernel(
        functools.partial(owner_body, tokens=tokens, modes=modes),
        "owner",
        "svv",
        (sds((blocks, back_rows), bf16),),
        [vmem((out_rows, LANES), f32), vmem((back_rows, LANES), f32)],
        10**6,
        10**6,
    )
    given = exchange(owner(doc_lengths, arrived, owned)[0])
    parts = lax.axis_size("ch")
    join = kernel(
        join_body,
        "join",
        "ssvvvvvvv",
        (sds((tokens, channels), f32), sds((parts, tokens), f32)),
        [vmem((back_rows, LANES), f32)],
        10**7,
        5 * 10**6,
    )
    gated, energy = join(doc_lengths, here, given, near, gate, edge, decay, residue, short_taps)
    energy = lax.all_to_all(energy.reshape(parts, 1, tokens), "ch", split_axis=0, concat_axis=0, tiled=True)
    scale = kernel(
        functools.partial(scale_body, width=float(channels * parts)),
        "scale",
        "vvv",
        (sds((tokens, channels), bf16),),
        [],
        10**6,
        2 * 10**6,
    )
    return scale(energy.reshape(parts, tokens), gated, gain.reshape(1, channels))[0]


def solution(mesh):
    placed = (
        P(None, ("gr", "gc"), "ch"),
        P(None, None, "ch"),
        P(None, "ch"),
        P(None, "ch"),
        P(),
        P("ch"),
    )
    return jax.shard_map(
        per_device, mesh=mesh, in_specs=placed, out_specs=P(("gr", "gc"), "ch"), check_vma=False
    )
```

time: 109 us -> 95.3 us (0.87)
  the two profiles are of different devices: /device:TPU:2 before, /device:TPU:1 now
where the time goes in v2:
time: 95.3 us; the launch traced here: 95 us
  blocking collectives  44.7 us (47%)
  Pallas kernels  21.4 us (22%)
  starting transfers between devices  20.4 us (21%)
  waiting for transfers between devices  7.45 us (8%)
    all_to_all x1, blocking collectives, exchange(): lax.all_to_all(block.reshape(blocks, 2, width // 2), ('gr', 'gc'), split_...  22.8 us
    all_to_all x1, blocking collectives, per_device(): lax.all_to_all(energy.reshape(parts, 1, tokens), 'ch', split_axis=0, conc...  21.8 us
    all_to_all x1, starting transfers between devices, exchange(): lax.all_to_all(block.reshape(blocks, 2, width // 2), ('gr', 'gc'), split_...  20.4 us
    pallas_call x1, Pallas kernels, per_device(): local(doc_lengths, here, far(features), far(prod), short_taps, decay, res...  9.56 us
    all_to_all x1, waiting for transfers between devices, exchange(): lax.all_to_all(block.reshape(blocks, 2, width // 2), ('gr', 'gc'), split_...  7.45 us
    pallas_call x1, Pallas kernels, per_device(): front(far(doc_lengths), here, far(features), far(short_taps), far(decay))  6.31 us
    pallas_call x1, Pallas kernels, per_device(): join(doc_lengths, here, given, near, gate, edge, decay, residue, short_taps)  2.94 us
  transfers between devices with their start and end apart: 1, of which 1 were waited for; matrix products, arithmetic and copies ran while one was open for 0% of the time, Pallas kernels for 10%

profile of v2, /device:TPU:1, one launch (start us, length us, event | category | flops | bytes accessed | tf_op | source)
XLA Modules:
  0.0 95.0 jit_solution(10236656883366754299)
XLA Ops:
  0.0 0.0 copy-start.5
  0.0 0.0 copy-start.1
  0.0 0.0 copy-start
  0.0 0.0 copy-start.2
  0.0 6.3 %front.1 = (bf16[128,768]{1,0:T(8,128)(2,1)S(1)}, bf16[128,2048]{1,0:T(8,128)(2,1)S(1)}) custom-call(s32[8]{0:T(128)} %lengths.5, s32[1]{0:T(128)} %bitcast.here, bf16[3,128,2048]{2,1,0:T(8,128)(2,1)} %feats_hbm.3, f32[3,7,2048]{2,1,0:T(8,128)} %taps.3, f32[16,2048]{1,0:T(8,128)} %decay.3), custom_call_target="tpu_custom_call" | custom-call | flops 10000000 | bytes 4000000 | tf_op jit(solution)/shard_map/front/pallas_call | solution.py:403
  6.3 0.0 copy-start.3
  6.4 0.8 reshape.25
  7.2 20.4 %all-to-all-start = ((bf16[128,2,384]{2,1,0:T(2,128)(2,1)}), bf16[128,2,384]{2,1,0:T(2,128)(2,1)S(1)}, u32[]{:S(2)}, u32[]{:S(2)}) async-start(bf16[128,2,384]{2,1,0:T(2,128)(2,1)} %reshape.25), calls=%async_computation | async-start | bytes 393216 | tf_op jit(solution)/shard_map/all_to_all | solution.py:347
  27.6 0.0 copy-done.3
  27.6 0.0 copy-done.5
  27.6 0.0 copy-done.1
  27.6 0.0 copy-done
  27.6 0.0 copy-done.2
  27.6 9.6 %local.1 = (bf16[128,2048]{1,0:T(8,128)(2,1)S(1)}, f32[128,2048]{1,0:T(8,128)S(1)}, f32[8,2048]{1,0:T(8,128)S(1)}, f32[848,128]{1,0:T(8,128)S(1)}) custom-call(s32[8]{0:T(128)S(1)} %copy-done.5, s32[1]{0:T(128)} %bitcast.here, bf16[3,128,2048]{2,1,0:T(8,128)(2,1)} %feats_hbm.3, bf16[128,2048]{1,0:T(8,128)(2,1)} %copy-done.3, f32[3,7,2048]{2,1,0:T(8,128)S(1)} %copy-done, ...), custom_call_target="tpu_custom_call" | custom-call | flops 100000000 | bytes 8000000 | tf_op jit(solution)/shard_map/local/pallas_call | solution.py:425
  37.2 7.5 %all-to-all-done = bf16[128,2,384]{2,1,0:T(2,128)(2,1)S(1)} async-done(((bf16[128,2,384]{2,1,0:T(2,128)(2,1)}), bf16[128,2,384]{2,1,0:T(2,128)(2,1)S(1)}, u32[]{:S(2)}, u32[]{:S(2)}) %all-to-all-start) | async-done | bytes 196640 | tf_op jit(solution)/shard_map/all_to_all | solution.py:347
  44.7 1.6 %owner.1 = bf16[128,512]{1,0:T(8,128)(2,1)S(1)} custom-call(s32[8]{0:T(128)S(1)} %copy-done.5, bf16[128,768]{1,0:T(8,128)(2,1)S(1)} %bitcast.10, f32[848,128]{1,0:T(8,128)S(1)} %get-tuple-element.15.owned), custom_call_target="tpu_custom_call" | custom-call | flops 1000000 | bytes 1000000 | tf_op jit(solution)/shard_map/owner/pallas_call | solution.py:435
  46.3 0.0 copy-start.4
  46.4 22.8 %all_to_all.15 = bf16[128,2,256]{2,1,0:T(2,128)(2,1)S(1)} all-to-all(bf16[128,2,256]{2,1,0:T(2,128)(2,1)S(1)} %reshape.27), channel_id=1, replica_groups=mesh['ch'=4,'gr'=16,'gc'=8] {'gr','gc'}, dimensions={0} | all-to-all | bytes 262144 | tf_op jit(solution)/shard_map/all_to_all | solution.py:347
  69.2 2.9 %join.1 = (f32[128,2048]{1,0:T(8,128)S(1)}, f32[4,128]{1,0:T(4,128)S(1)}) custom-call(s32[8]{0:T(128)S(1)} %copy-done.5, s32[1]{0:T(128)} %bitcast.here, bf16[128,512]{1,0:T(8,128)(2,1)S(1)} %bitcast.11, f32[128,2048]{1,0:T(8,128)S(1)} %get-tuple-element.16.near, bf16[128,2048]{1,0:T(8,128)(2,1)S(1)} %get-tuple-element.17.gate, ...), custom_call_target="tpu_custom_call" | custom-call | flops 10000000 | bytes 5000000 | tf_op jit(solution)/shard_map/join/pallas_call | solution.py:446
  72.2 21.8 %all_to_all.16 = f32[4,1,128]{2,1,0:T(1,128)S(1)} all-to-all(f32[4,1,128]{2,1,0:T(1,128)S(1)} %bitcast.14), channel_id=1, replica_groups=mesh['ch'=4,'gr'=16,'gc'=8] {'ch'}, dimensions={0} | all-to-all | bytes 4096 | tf_op jit(solution)/shard_map/all_to_all | solution.py:447
  94.0 0.0 copy-done.4
  94.0 1.0 %scale.1 = bf16[128,2048]{1,0:T(8,128)(2,1)} custom-call(f32[4,128]{1,0:T(4,128)S(1)} %bitcast.13, f32[128,2048]{1,0:T(8,128)S(1)} %get-tuple-element.20.gated, f32[1,2048]{1,0:T(1,128)S(1)} %bitcast.12), custom_call_target="tpu_custom_call" | custom-call | flops 1000000 | bytes 2000000 | tf_op jit(solution)/shard_map/scale/pallas_call | solution.py:457
  (3 shorter events, 0.1 us)
Async XLA Ops:
  0.0 27.6 %copy-start.5 = (s32[8]{0:T(128)S(1)}, s32[8]{0:T(128)}, u32[]{:S(2)}) copy-start(s32[8]{0:T(128)} %lengths.5) | copy-start | bytes 100
  0.0 27.6 %copy-start.1 = (f32[16,2048]{1,0:T(8,128)S(1)}, f32[16,2048]{1,0:T(8,128)}, u32[]{:S(2)}) copy-start(f32[16,2048]{1,0:T(8,128)} %decay.3) | copy-start | bytes 393220
  0.0 27.6 %copy-start = (f32[3,7,2048]{2,1,0:T(8,128)S(1)}, f32[3,7,2048]{2,1,0:T(8,128)}, u32[]{:S(2)}) copy-start(f32[3,7,2048]{2,1,0:T(8,128)} %taps.3) | copy-start | bytes 516100
  0.0 27.6 %copy-start.2 = (f32[16,2048]{1,0:T(8,128)S(1)}, f32[16,2048]{1,0:T(8,128)}, u32[]{:S(2)}) copy-start(f32[16,2048]{1,0:T(8,128)} %residue.3) | copy-start | bytes 393220
  6.3 21.3 %copy-start.3 = (bf16[128,2048]{1,0:T(8,128)(2,1)}, bf16[128,2048]{1,0:T(8,128)(2,1)S(1)}, u32[]{:S(2)}) copy-start(bf16[128,2048]{1,0:T(8,128)(2,1)S(1)} %get-tuple-element.14.prod_hbm) | copy-start | bytes 1572868
  7.2 37.5 %all-to-all-start = ((bf16[128,2,384]{2,1,0:T(2,128)(2,1)}), bf16[128,2,384]{2,1,0:T(2,128)(2,1)S(1)}, u32[]{:S(2)}, u32[]{:S(2)}) async-start(bf16[128,2,384]{2,1,0:T(2,128)(2,1)} %reshape.25), calls=%async_computation | async-start | bytes 393216 | tf_op jit(solution)/shard_map/all_to_all | solution.py:347
  46.3 47.7 %copy-start.4 = (f32[2048]{0:T(1024)S(1)}, f32[2048]{0:T(1024)}, u32[]{:S(2)}) copy-start(f32[2048]{0:T(1024)} %param.11) | copy-start | bytes 24580

commit v3 on v2

v3 whole, which is shorter than its diff:
```python
import functools

import jax
import jax.numpy as jnp
from jax import lax
from jax.experimental import pallas as pl
from jax.experimental.pallas import tpu as pltpu
from jax.sharding import PartitionSpec as P


LANES = 128
TAPS = 7
HEAD = TAPS - 1
SUB = 8
VMEM_LIMIT = 12 * 1024 * 1024


def doc_start(lengths, position):
    start, found = jnp.int32(0), jnp.zeros_like(position)
    for doc in range(lengths.shape[0]):
        found = jnp.where(position >= start, jnp.maximum(found, start), found)
        start = start + lengths[doc]
    return found


def short_conv(shifts, x, taps):
    tokens = x.shape[0]
    moved = jnp.dot(shifts, x, preferred_element_type=jnp.float32)
    total = x.astype(jnp.float32) * taps(0)
    for i in range(1, TAPS):
        total = total + moved[(i - 1) * tokens : i * tokens] * taps(i)
    return total.astype(jnp.bfloat16)


def rows_of(shape, dim=0):
    return lax.broadcasted_iota(jnp.int32, shape, dim)


def powers(ratio):
    square = ratio * ratio
    fourth = square * square
    return ratio, square, fourth, fourth * fourth


def spread(row, rows=SUB):
    return jnp.broadcast_to(row, (rows, row.shape[1]))


def fill_shifts(shifts, lengths, first_token):
    tokens = shifts.shape[1]
    row = rows_of((tokens, tokens))
    column = rows_of((tokens, tokens), 1)
    position = row + first_token
    reach = position - doc_start(lengths, position)
    for i in range(1, TAPS):
        hit = (column == row - i) & (reach >= i)
        shifts[(i - 1) * tokens : i * tokens, :] = jnp.where(hit, 1.0, 0.0).astype(jnp.bfloat16)


def front_body(
    lengths_hbm, here, feats_hbm, taps_hbm, decay_hbm, msg, prod_hbm, stage, feats, taps, decay, prod, shifts, lengths, sems
):
    pair, tokens, channels = feats.shape
    modes = decay.shape[0]
    groups = channels // LANES
    wide = 2 * LANES
    count = channels // wide

    def fetched(block, k):
        lanes = slice(block * wide, (block + 1) * wide)
        at = 3 + count + block * pair + k
        return pltpu.make_async_copy(feats_hbm.at[2 * k, :, lanes], feats.at[k, :, lanes], sems.at[at])

    def stored(block):
        lanes = slice(block * wide, (block + 1) * wide)
        return pltpu.make_async_copy(prod.at[:, lanes], prod_hbm.at[:, lanes], sems.at[3 + block])

    counted = pltpu.make_async_copy(lengths_hbm, lengths, sems.at[0])
    others = (
        pltpu.make_async_copy(taps_hbm, taps, sems.at[1]),
        pltpu.make_async_copy(decay_hbm, decay, sems.at[2]),
    )
    counted.start()
    for k in range(pair):
        fetched(0, k).start()
    for copy in others:
        copy.start()
    for block in range(1, count):
        for k in range(pair):
            fetched(block, k).start()
    states = groups * modes
    used = states + 2 * pair * HEAD * groups
    if used < stage.shape[0]:
        stage[used:, :] = jnp.zeros((stage.shape[0] - used, LANES), jnp.float32)
    counted.wait()
    fill_shifts(shifts, lengths, here[0] * tokens)
    for copy in others:
        copy.wait()
    for block in range(count):
        lanes = slice(block * wide, (block + 1) * wide)
        for k in range(pair):
            fetched(block, k).wait()
        first, third = (
            short_conv(shifts[...], feats[k, :, lanes], lambda i, k=k: taps[2 * k, i : i + 1, lanes])
            for k in range(pair)
        )
        product = first.astype(jnp.float32) * third.astype(jnp.float32)
        product = jnp.where(rows_of((tokens, wide)) >= HEAD, product, 0.0).astype(jnp.bfloat16)
        prod[:, lanes] = product
        stored(block).start()
        values = product.astype(jnp.float32)
        for half in range(wide // LANES):
            j = block * (wide // LANES) + half
            mine = slice(j * LANES, (j + 1) * LANES)
            v = values[:, half * LANES : (half + 1) * LANES]
            tables = powers(jnp.exp(-decay[:, mine]))
            for m in range(modes):
                one, two, four, eight = (spread(t[m : m + 1]) for t in tables)
                state = v[0:SUB]
                for q in range(1, tokens // SUB):
                    state = state * eight + v[q * SUB : (q + 1) * SUB]
                state = state * four + pltpu.roll(state, SUB - 4, 0)
                state = state * two + pltpu.roll(state, SUB - 2, 0)
                state = state * one + pltpu.roll(state, SUB - 1, 0)
                stage[j * modes + m : j * modes + m + 1, :] = state[0:1]
            at = states
            for k, low in ((0, True), (1, True), (0, False), (1, False)):
                part = feats[k, tokens - 2 * SUB : tokens, mine] if low else feats[k, 0 : 2 * SUB, mine]
                part = part.astype(jnp.float32)
                skip = 2 * SUB - HEAD if low else 0
                for r in range(HEAD):
                    stage[at + r * groups + j : at + r * groups + j + 1, :] = part[skip + r : skip + r + 1]
                at += HEAD * groups
    for c in range(stage.shape[0] // LANES):
        msg[:, c * LANES : (c + 1) * LANES] = stage[c * LANES : (c + 1) * LANES, :].T.astype(jnp.bfloat16)
    for block in range(count):
        stored(block).wait()


def gate_body(lengths, here, feats_hbm, taps, decay, residue, gate, ends, owned, feats, shifts, sems):
    _, tokens, channels = feats.shape
    modes = decay.shape[0]
    groups = channels // LANES
    wide = 2 * LANES
    copies = [
        pltpu.make_async_copy(feats_hbm.at[b], feats.at[b], sems.at[b]) for b in (1, 0, 2)
    ]
    for copy in copies:
        copy.start()
    fill_shifts(shifts, lengths, here[0] * tokens)
    states = groups * modes
    chosen = rows_of((modes, LANES), 1) == here[0]
    chosen_taps = rows_of((TAPS, LANES), 1) == here[0]
    for j in range(groups):
        mine = slice(j * LANES, (j + 1) * LANES)
        at = slice(j * modes, (j + 1) * modes)
        pick = jnp.sum(jnp.where(chosen, decay[:, mine], 0.0), axis=1, keepdims=True)
        owned[at, :] = jnp.broadcast_to(pick, (modes, LANES))
        for b in (0, 2):
            pick = jnp.sum(jnp.where(chosen_taps, taps[b, :, mine], 0.0), axis=1, keepdims=True)
            pick = jnp.broadcast_to(pick, (TAPS, LANES))
            for i in range(TAPS):
                to = states + (b // 2 * TAPS + i) * groups + j
                owned[to : to + 1, :] = pick[i : i + 1]
    for copy in copies:
        copy.wait()
    for b in range(3):
        ends[b] = feats[b, tokens - 2 * SUB : tokens, :].astype(jnp.float32)[SUB:].astype(jnp.bfloat16)
    for block in range(channels // wide):
        lanes = slice(block * wide, (block + 1) * wide)
        gate[:, lanes] = short_conv(shifts[...], feats[1, :, lanes], lambda i: taps[1, i : i + 1, lanes])


def near_body(
    lengths, here, turn, halo, feats_hbm, prod_hbm, taps, decay, residue, near, top, table, prod, front, last, sems
):
    tokens, channels = near.shape
    modes = decay.shape[0]
    groups = channels // LANES
    chunks = tokens // SUB
    copies = [
        pltpu.make_async_copy(feats_hbm.at[b, 0 : 2 * SUB, :], front.at[b], sems.at[b]) for b in range(3)
    ]
    copies.append(pltpu.make_async_copy(prod_hbm, prod, sems.at[3]))
    for copy in copies:
        copy.start()
    last[...] = halo[...].astype(jnp.float32)
    inside = rows_of((SUB, LANES))
    steps = inside.astype(jnp.float32)
    position = inside + here[0] * tokens
    reach = position - doc_start(lengths, position)
    for copy in copies:
        copy.wait()

    def head(b, mine):
        now = front[b, :, mine].astype(jnp.float32)[0:SUB]
        before = last[b, :, mine]
        total = now * taps[b, 0:1, mine]
        for i in range(1, TAPS):
            moved = jnp.where(inside < i, pltpu.roll(before, i, 0), pltpu.roll(now, i, 0))
            total = total + jnp.where(reach >= i, moved * taps[b, i : i + 1, mine], 0.0)
        return total.astype(jnp.bfloat16).astype(jnp.float32)

    def group(j, carry):
        mine = pl.ds(pl.multiple_of(j * LANES, LANES), LANES)
        top[:, mine] = head(1, mine)
        first = (head(0, mine) * head(2, mine)).astype(jnp.bfloat16).astype(jnp.float32)
        sums = [jnp.zeros((SUB, LANES), jnp.float32) for _ in range(chunks)]
        rates = decay[:, mine]
        weights = residue[:, mine] * jnp.sqrt(2.0 * rates)
        eights = jnp.exp(-SUB * rates)
        for m in range(modes):
            step = spread(eights[m : m + 1])
            wave = weights[m : m + 1] * jnp.exp(-rates[m : m + 1] * steps)
            for q in range(chunks):
                sums[q] = sums[q] + wave
                if q + 1 < chunks:
                    wave = wave * step
        for q in range(chunks):
            table[q * SUB : (q + 1) * SUB, :] = sums[q]
        values = prod[:, mine].astype(jnp.float32)
        values = [values[q * SUB : (q + 1) * SUB] for q in range(chunks)]
        values[0] = jnp.where(inside < HEAD, first, values[0])
        total = [jnp.zeros((SUB, LANES), jnp.float32) for _ in range(chunks)]
        for k in range(SUB):
            moved = values
            if k:
                turned = [pltpu.roll(v, k, 0) for v in values]
                low = inside < k
                moved = [jnp.where(low, turned[q - 1] if q else 0.0, turned[q]) for q in range(chunks)]
            for d in range(chunks):
                factor = spread(table[d * SUB + k : d * SUB + k + 1, :])
                for q in range(d, chunks):
                    total[q] = total[q] + factor * moved[q - d]
        for q in range(chunks):
            near[q * SUB : (q + 1) * SUB, mine] = total[q]
        return carry

    lax.fori_loop(0, groups, group, 0)


def owner_body(lengths, arrived, owned, back, turn, stage, out, *, tokens, modes):
    blocks = arrived.shape[0]
    groups = owned.shape[0] // (modes + 2 * TAPS)
    states = modes * groups
    for c in range(stage.shape[0] // LANES):
        stage[c * LANES : (c + 1) * LANES, :] = arrived[:, c * LANES : (c + 1) * LANES].astype(jnp.float32).T
    lane = rows_of((groups, blocks), 1)

    def part(k, r):
        at = states + (k * HEAD + r) * groups
        return stage[at : at + groups, :]

    def before(k, r):
        return jnp.where(lane >= 1, pltpu.roll(part(k, r), 1, 1), 0.0)

    reach = []
    for r in range(HEAD):
        position = lane * tokens + r
        reach.append(position - doc_start(lengths, position))
    heads = []
    for k in range(2):
        ext = [before(k, r) for r in range(HEAD)] + [part(2 + k, r) for r in range(HEAD)]
        found = []
        for r in range(HEAD):
            total = jnp.zeros((groups, blocks), jnp.float32)
            for i in range(TAPS):
                at = states + (k * TAPS + i) * groups
                term = owned[at : at + groups, :] * ext[HEAD + r - i]
                total = total + jnp.where(reach[r] >= i, term, 0.0)
            found.append(total.astype(jnp.bfloat16).astype(jnp.float32))
        heads.append(found)
    products = [(a * b).astype(jnp.bfloat16).astype(jnp.float32) for a, b in zip(*heads)]
    lane = rows_of((modes, blocks), 1)
    for j in range(groups):
        at = slice(j * modes, (j + 1) * modes)
        rate = owned[at, :]
        ratio = jnp.exp(-rate)
        head = spread(products[0][j : j + 1], modes)
        for r in range(1, HEAD):
            head = head * ratio + spread(products[r][j : j + 1], modes)
        total = stage[at, :] + jnp.exp(-rate * (tokens - HEAD)) * head
        decline = jnp.exp(-rate * tokens)
        distance = 1
        while distance < blocks:
            shifted = jnp.where(lane >= distance, pltpu.roll(total, distance, 1), 0.0)
            total = total + decline * shifted
            decline = decline * decline
            distance *= 2
        out[at, :] = jnp.where(lane >= 1, pltpu.roll(total, 1, 1), 0.0)
    for c in range(states // LANES):
        back[:, c * LANES : (c + 1) * LANES] = out[c * LANES : (c + 1) * LANES, :].T.astype(jnp.bfloat16)
    turn[...] = jnp.zeros(turn.shape, jnp.float32)


def join_body(back, near, gate, top, decay, residue, gated, energy, stage):
    tokens, channels = near.shape
    modes = decay.shape[0]
    groups = channels // LANES
    chunks = tokens // SUB
    for c in range(stage.shape[0] // LANES):
        stage[c * LANES : (c + 1) * LANES, :] = back[:, c * LANES : (c + 1) * LANES].astype(jnp.float32).T
    inside = rows_of((SUB, LANES))
    odd, pair, quad = ((inside & bit) != 0 for bit in (1, 2, 4))
    squares = [jnp.zeros((SUB, LANES), jnp.float32) for _ in range(chunks)]
    for j in range(groups):
        mine = slice(j * LANES, (j + 1) * LANES)
        total = [near[q * SUB : (q + 1) * SUB, mine] for q in range(chunks)]
        rates = decay[:, mine]
        tables = powers(jnp.exp(-rates))
        start = stage[j * modes : (j + 1) * modes, :] * residue[:, mine] * jnp.sqrt(2.0 * rates)
        start = start * tables[0]
        for m in range(modes):
            one, two, four, eight = (spread(t[m : m + 1]) for t in tables)
            wave = spread(start[m : m + 1])
            wave = jnp.where(odd, wave * one, wave)
            wave = jnp.where(pair, wave * two, wave)
            wave = jnp.where(quad, wave * four, wave)
            for q in range(chunks):
                total[q] = total[q] + wave
                if q + 1 < chunks:
                    wave = wave * eight
        gates = gate[:, mine].astype(jnp.float32)
        for q in range(chunks):
            g = gates[q * SUB : (q + 1) * SUB] if q else top[:, mine]
            value = g * total[q].astype(jnp.bfloat16).astype(jnp.float32)
            gated[q * SUB : (q + 1) * SUB, mine] = value
            squares[q] = squares[q] + value * value
    summed = jnp.sum(jnp.concatenate(squares, axis=0), axis=1, keepdims=True)
    energy[...] = jnp.broadcast_to(summed, (tokens, LANES)).T[0:1, :]


def scale_body(energy, gated, gain, mixed, *, width):
    tokens, channels = gated.shape
    scaling = lax.rsqrt(jnp.sum(energy[...], axis=0, keepdims=True) / width + 1e-06)
    scaling = jnp.broadcast_to(scaling, (LANES, tokens)).T
    for j in range(channels // LANES):
        mine = slice(j * LANES, (j + 1) * LANES)
        mixed[:, mine] = (gated[:, mine] * scaling * gain[:, mine]).astype(jnp.bfloat16)


def exchange(block):
    blocks, width = block.shape
    moved = lax.all_to_all(
        block.reshape(blocks, 2, width // 2), ("gr", "gc"), split_axis=0, concat_axis=0, tiled=True
    )
    return moved.reshape(blocks, width)


def padded(rows):
    return -(-rows // (2 * LANES)) * 2 * LANES


def kernel(body, name, kinds, outs, scratch, flops, moved, given="vvvv"):
    spaces = {"s": pltpu.SMEM, "v": pltpu.VMEM, "h": pltpu.HBM}
    return pl.pallas_call(
        body,
        out_shape=outs,
        in_specs=[pl.BlockSpec(memory_space=spaces[k]) for k in kinds],
        out_specs=tuple(pl.BlockSpec(memory_space=spaces[k]) for k, _ in zip(given, outs)),
        scratch_shapes=scratch,
        compiler_params=pltpu.CompilerParams(vmem_limit_bytes=VMEM_LIMIT),
        cost_estimate=pl.CostEstimate(flops=flops, bytes_accessed=moved, transcendentals=0),
        name=name,
    )


def per_device(features, short_taps, decay, residue, doc_lengths, gain):
    _, tokens, channels = features.shape
    modes = decay.shape[0]
    blocks = lax.axis_size(("gr", "gc"))
    groups = channels // LANES
    states = groups * modes
    here = lax.axis_index(("gr", "gc")).astype(jnp.int32).reshape(1)
    f32, bf16 = jnp.float32, jnp.bfloat16
    sds = jax.ShapeDtypeStruct
    vmem = pltpu.VMEM
    out_rows = padded(states + 4 * HEAD * groups)
    wide = 2 * LANES
    front = kernel(
        front_body,
        "front",
        "hshhh",
        (sds((blocks, out_rows), bf16), sds((tokens, channels), bf16)),
        [
            vmem((out_rows, LANES), f32),
            vmem((2, tokens, channels), bf16),
            vmem(short_taps.shape, f32),
            vmem(decay.shape, f32),
            vmem((tokens, channels), bf16),
            vmem((HEAD * tokens, tokens), bf16),
            pltpu.SMEM(doc_lengths.shape, jnp.int32),
            pltpu.SemaphoreType.DMA((3 + 3 * (channels // wide),)),
        ],
        10**7,
        4 * 10**6,
        "vh",
    )
    far = functools.partial(pltpu.with_memory_space_constraint, memory_space=pltpu.HBM)
    msg, prod = front(far(doc_lengths), here, far(features), far(short_taps), far(decay))
    arrived = exchange(msg)
    gating = kernel(
        gate_body,
        "gate",
        "sshvvv",
        (
            sds((tokens, channels), bf16),
            sds((3, SUB, channels), bf16),
            sds((states + 2 * TAPS * groups, LANES), f32),
        ),
        [
            vmem(features.shape, bf16),
            vmem((HEAD * tokens, tokens), bf16),
            pltpu.SemaphoreType.DMA((3,)),
        ],
        5 * 10**7,
        4 * 10**6,
    )
    gate, ends, owned = gating(doc_lengths, here, far(features), short_taps, decay, residue)
    halo = lax.ppermute(ends, ("gr", "gc"), [(i, i + 1) for i in range(blocks - 1)])
    owner = kernel(
        functools.partial(owner_body, tokens=tokens, modes=modes),
        "owner",
        "svv",
        (sds((blocks, states), bf16), sds((SUB, LANES), f32)),
        [vmem((out_rows, LANES), f32), vmem((states, LANES), f32)],
        10**6,
        10**6,
    )
    back, turn = owner(doc_lengths, arrived, owned)
    given = exchange(back)
    local = kernel(
        near_body,
        "near",
        "ssvvhhvvv",
        (sds((tokens, channels), f32), sds((SUB, channels), f32)),
        [
            vmem((tokens, LANES), f32),
            vmem((tokens, channels), bf16),
            vmem((3, 2 * SUB, channels), bf16),
            vmem((3, SUB, channels), f32),
            pltpu.SemaphoreType.DMA((4,)),
        ],
        10**8,
        8 * 10**6,
    )
    near, top = local(doc_lengths, here, turn, halo, far(features), far(prod), short_taps, decay, residue)
    join = kernel(
        join_body,
        "join",
        "vvvvvv",
        (sds((tokens, channels), f32), sds((1, tokens), f32)),
        [vmem((states, LANES), f32)],
        10**7,
        5 * 10**6,
    )
    gated, energy = join(given, near, gate, top, decay, residue)
    energy = lax.all_gather(energy, "ch", tiled=True)
    scale = kernel(
        functools.partial(scale_body, width=float(channels * lax.axis_size("ch"))),
        "scale",
        "vvv",
        (sds((tokens, channels), bf16),),
        [],
        10**6,
        2 * 10**6,
    )
    return scale(energy, gated, gain.reshape(1, channels))[0]


def solution(mesh):
    placed = (
        P(None, ("gr", "gc"), "ch"),
        P(None, None, "ch"),
        P(None, "ch"),
        P(None, "ch"),
        P(),
        P("ch"),
    )
    return jax.shard_map(
        per_device, mesh=mesh, in_specs=placed, out_specs=P(("gr", "gc"), "ch"), check_vma=False
    )
```

time: 95.3 us -> 98.9 us (1.038)
  the two profiles are of different devices: /device:TPU:1 before, /device:TPU:7 now
where the time goes in v3:
time: 98.9 us; the launch traced here: 98.6 us
  starting transfers between devices  33.2 us (34%)
  waiting for transfers between devices  24.1 us (24%)
  Pallas kernels  22.6 us (23%)
  blocking collectives  16.3 us (16%)
  local copies, waits for them, and re-layouts  2.22 us (2%)
    all_to_all x2, starting transfers between devices, exchange(): lax.all_to_all(block.reshape(blocks, 2, width // 2), ('gr', 'gc'), split_...  30 us
    all_gather x1, blocking collectives, per_device(): energy = lax.all_gather(energy, 'ch', tiled=True)  16.3 us
    all_to_all x2, waiting for transfers between devices, exchange(): lax.all_to_all(block.reshape(blocks, 2, width // 2), ('gr', 'gc'), split_...  12.5 us
    ppermute x1, waiting for transfers between devices, per_device(): lax.ppermute(ends, ('gr', 'gc'), [(i, i + 1) for i in range(blocks - 1)])  11.7 us
    pallas_call x1, Pallas kernels, per_device(): local(doc_lengths, here, turn, halo, far(features), far(prod), short_taps...  8.49 us
    pallas_call x1, Pallas kernels, per_device(): front(far(doc_lengths), here, far(features), far(short_taps), far(decay))  6.34 us
    ppermute x1, starting transfers between devices, per_device(): lax.ppermute(ends, ('gr', 'gc'), [(i, i + 1) for i in range(blocks - 1)])  3.28 us
    pallas_call x1, Pallas kernels, per_device(): gating(doc_lengths, here, far(features), short_taps, decay, residue)  2.92 us
  transfers between devices with their start and end apart: 3, of which 2 were waited for; matrix products, arithmetic and copies ran while one was open for 0% of the time, Pallas kernels for 12%

profile of v3, /device:TPU:7, one launch (start us, length us, event | category | flops | bytes accessed | tf_op | source)
XLA Modules:
  0.0 98.6 jit_solution(7360917710873038097)
XLA Ops:
  0.0 0.0 copy-start.5
  0.0 0.0 copy-start
  0.0 0.0 copy-start.1
  0.0 0.0 copy-start.2
  0.0 6.3 %front.1 = (bf16[128,768]{1,0:T(8,128)(2,1)S(1)}, bf16[128,2048]{1,0:T(8,128)(2,1)S(1)}) custom-call(s32[8]{0:T(128)} %lengths.5, s32[1]{0:T(128)} %bitcast.here, bf16[3,128,2048]{2,1,0:T(8,128)(2,1)} %feats_hbm.5, f32[3,7,2048]{2,1,0:T(8,128)} %taps.3, f32[16,2048]{1,0:T(8,128)} %decay.5), custom_call_target="tpu_custom_call" | custom-call | flops 10000000 | bytes 4000000 | tf_op jit(solution)/shard_map/front/pallas_call | solution.py:400
  6.4 0.0 copy-start.3
  6.4 0.8 copy-done.3
  7.2 0.7 reshape.19
  7.9 19.4 %all-to-all-start = ((bf16[128,2,384]{2,1,0:T(2,128)(2,1)}), bf16[128,2,384]{2,1,0:T(2,128)(2,1)S(1)}, u32[]{:S(2)}, u32[]{:S(2)}) async-start(bf16[128,2,384]{2,1,0:T(2,128)(2,1)} %reshape.19), calls=%async_computation | async-start | bytes 393216 | tf_op jit(solution)/shard_map/all_to_all | solution.py:344
  27.3 0.0 copy-done.5
  27.3 0.0 copy-done
  27.3 0.0 copy-done.1
  27.3 0.0 copy-done.2
  27.4 2.9 %gate.1 = (bf16[128,2048]{1,0:T(8,128)(2,1)S(1)}, bf16[3,8,2048]{2,1,0:T(8,128)(2,1)S(1)}, f32[480,128]{1,0:T(8,128)S(1)}) custom-call(s32[8]{0:T(128)S(1)} %copy-done.5, s32[1]{0:T(128)} %bitcast.here, bf16[3,128,2048]{2,1,0:T(8,128)(2,1)} %feats_hbm.5, f32[3,7,2048]{2,1,0:T(8,128)S(1)} %copy-done.1, f32[16,2048]{1,0:T(8,128)S(1)} %copy-done, ...), custom_call_target="tpu_custom_call" | custom-call | flops 50000000 | bytes 4000000 | tf_op jit(solution)/shard_map/gate/pallas_call | solution.py:419
  30.3 12.4 %all-to-all-done = bf16[128,2,384]{2,1,0:T(2,128)(2,1)S(1)} async-done(((bf16[128,2,384]{2,1,0:T(2,128)(2,1)}), bf16[128,2,384]{2,1,0:T(2,128)(2,1)S(1)}, u32[]{:S(2)}, u32[]{:S(2)}) %all-to-all-start) | async-done | bytes 196640 | tf_op jit(solution)/shard_map/all_to_all | solution.py:344
  42.8 1.5 %owner.1 = (bf16[128,256]{1,0:T(8,128)(2,1)S(1)}, f32[8,128]{1,0:T(8,128)S(1)}) custom-call(s32[8]{0:T(128)S(1)} %copy-done.5, bf16[128,768]{1,0:T(8,128)(2,1)S(1)} %bitcast.10, f32[480,128]{1,0:T(8,128)S(1)} %get-tuple-element.17.owned), custom_call_target="tpu_custom_call" | custom-call | flops 1000000 | bytes 1000000 | tf_op jit(solution)/shard_map/owner/pallas_call | solution.py:430
  44.3 0.6 reshape.21
  44.9 10.6 %all-to-all-start.1 = ((bf16[128,2,128]{2,1,0:T(2,128)(2,1)}), bf16[128,2,128]{2,1,0:T(2,128)(2,1)S(1)}, u32[]{:S(2)}, u32[]{:S(2)}) async-start(bf16[128,2,128]{2,1,0:T(2,128)(2,1)} %reshape.21), calls=%async_computation.1 | async-start | bytes 131072 | tf_op jit(solution)/shard_map/all_to_all | solution.py:344
  55.5 3.3 %collective-permute-start = (bf16[3,8,2048]{2,1,0:T(8,128)(2,1)S(1)}, bf16[3,8,2048]{2,1,0:T(8,128)(2,1)S(1)}, u32[]{:S(2)}, u32[]{:S(2)}) collective-permute-start(bf16[3,8,2048]{2,1,0:T(8,128)(2,1)S(1)} %get-tuple-element.20), channel_id=1, source_target_pairs={{0,1},{1,2},{2,3},{3,4},{4,5},{5,6},{6,7},{7,8},{8,9},{9,10},{10,1... | collective-permute-start | bytes 294920 | tf_op jit(solution)/shard_map/ppermute | solution.py:420
  58.8 11.7 %collective-permute-done.halo = bf16[3,8,2048]{2,1,0:T(8,128)(2,1)S(1)} collective-permute-done((bf16[3,8,2048]{2,1,0:T(8,128)(2,1)S(1)}, bf16[3,8,2048]{2,1,0:T(8,128)(2,1)S(1)}, u32[]{:S(2)}, u32[]{:S(2)}) %collective-permute-start) | collective-permute-done | bytes 98336 | tf_op jit(solution)/shard_map/ppermute | solution.py:420
  70.4 8.5 %near.1 = (f32[128,2048]{1,0:T(8,128)S(1)}, f32[8,2048]{1,0:T(8,128)S(1)}) custom-call(s32[8]{0:T(128)S(1)} %copy-done.5, s32[1]{0:T(128)} %bitcast.here, f32[8,128]{1,0:T(8,128)S(1)} %get-tuple-element.19.turn, bf16[3,8,2048]{2,1,0:T(8,128)(2,1)S(1)} %collective-permute-done.halo, bf16[3,128,2048]{2,1,0:T(8,128)(2,1)} %feats_hbm.5, ...), custom_call_target="tpu_custom_call" | custom-call | flops 100000000 | bytes 8000000 | tf_op jit(solution)/shard_map/near/pallas_call | solution.py:447
  78.9 0.0 copy-start.4
  79.0 0.0 all-to-all-done.1
  79.0 2.3 %join.1 = (f32[128,2048]{1,0:T(8,128)S(1)}, f32[1,128]{1,0:T(1,128)S(1)}) custom-call(bf16[128,256]{1,0:T(8,128)(2,1)S(1)} %bitcast.11, f32[128,2048]{1,0:T(8,128)S(1)} %get-tuple-element.22.near, bf16[128,2048]{1,0:T(8,128)(2,1)S(1)} %get-tuple-element.23.gate, f32[8,2048]{1,0:T(8,128)S(1)} %get-tuple-element.24.top, f32[16,2048]{1,0:T(8,128)S(1)} %copy-done, ...), custom_call_target="tpu_custom_call" | custom-call | flops 10000000 | bytes 5000000 | tf_op jit(solution)/shard_map/join/pallas_call | solution.py:457
  81.3 16.3 %all-gather = f32[4,1,128]{2,1,0:T(1,128)S(1)} all-gather(f32[1,1,128]{2,1,0:T(1,128)S(1)} %bitcast.14), channel_id=1, replica_groups=mesh['ch'=4,'gr'=16,'gc'=8] {'ch'}, dimensions={0}, use_global_device_ids=true | all-gather | bytes 2560 | tf_op jit(solution)/shard_map/all_gather | solution.py:458
  97.6 0.0 copy-done.4
  97.6 1.0 %scale.1 = bf16[128,2048]{1,0:T(8,128)(2,1)} custom-call(f32[4,128]{1,0:T(4,128)S(1)} %bitcast.13, f32[128,2048]{1,0:T(8,128)S(1)} %get-tuple-element.26.gated, f32[1,2048]{1,0:T(1,128)S(1)} %bitcast.12), custom_call_target="tpu_custom_call" | custom-call | flops 1000000 | bytes 2000000 | tf_op jit(solution)/shard_map/scale/pallas_call | solution.py:468
  (2 shorter events, 0.0 us)
Async XLA Ops:
  0.0 27.3 %copy-start.5 = (s32[8]{0:T(128)S(1)}, s32[8]{0:T(128)}, u32[]{:S(2)}) copy-start(s32[8]{0:T(128)} %lengths.5) | copy-start | bytes 100
  0.0 27.3 %copy-start = (f32[16,2048]{1,0:T(8,128)S(1)}, f32[16,2048]{1,0:T(8,128)}, u32[]{:S(2)}) copy-start(f32[16,2048]{1,0:T(8,128)} %decay.5) | copy-start | bytes 393220
  0.0 27.3 %copy-start.1 = (f32[3,7,2048]{2,1,0:T(8,128)S(1)}, f32[3,7,2048]{2,1,0:T(8,128)}, u32[]{:S(2)}) copy-start(f32[3,7,2048]{2,1,0:T(8,128)} %taps.3) | copy-start | bytes 516100
  0.0 27.3 %copy-start.2 = (f32[16,2048]{1,0:T(8,128)S(1)}, f32[16,2048]{1,0:T(8,128)}, u32[]{:S(2)}) copy-start(f32[16,2048]{1,0:T(8,128)} %residue.5) | copy-start | bytes 393220
  6.4 0.8 copy-start.3
  7.9 34.8 %all-to-all-start = ((bf16[128,2,384]{2,1,0:T(2,128)(2,1)}), bf16[128,2,384]{2,1,0:T(2,128)(2,1)S(1)}, u32[]{:S(2)}, u32[]{:S(2)}) async-start(bf16[128,2,384]{2,1,0:T(2,128)(2,1)} %reshape.19), calls=%async_computation | async-start | bytes 393216 | tf_op jit(solution)/shard_map/all_to_all | solution.py:344
  44.9 34.0 %all-to-all-start.1 = ((bf16[128,2,128]{2,1,0:T(2,128)(2,1)}), bf16[128,2,128]{2,1,0:T(2,128)(2,1)S(1)}, u32[]{:S(2)}, u32[]{:S(2)}) async-start(bf16[128,2,128]{2,1,0:T(2,128)(2,1)} %reshape.21), calls=%async_computation.1 | async-start | bytes 131072 | tf_op jit(solution)/shard_map/all_to_all | solution.py:344
  55.5 15.0 %collective-permute-start = (bf16[3,8,2048]{2,1,0:T(8,128)(2,1)S(1)}, bf16[3,8,2048]{2,1,0:T(8,128)(2,1)S(1)}, u32[]{:S(2)}, u32[]{:S(2)}) collective-permute-start(bf16[3,8,2048]{2,1,0:T(8,128)(2,1)S(1)} %get-tuple-element.20), channel_id=1, source_target_pairs={{0,1},{1,2},{2,3},{3,4},{4,5},{5,6},{6,7},{7,8},{8,9},{9,10},{10,1... | collective-permute-start | bytes 294920 | tf_op jit(solution)/shard_map/ppermute | solution.py:420
  78.9 18.6 %copy-start.4 = (f32[2048]{0:T(1024)S(1)}, f32[2048]{0:T(1024)}, u32[]{:S(2)}) copy-start(f32[2048]{0:T(1024)} %param.11) | copy-start | bytes 24580

commit v4 on v2

--- a/solution.py
+++ b/solution.py
@@ -57,34 +57,28 @@
         shifts[(i - 1) * tokens : i * tokens, :] = jnp.where(hit, 1.0, 0.0).astype(jnp.bfloat16)
 
 
-def front_body(
-    lengths_hbm, here, feats_hbm, taps_hbm, decay_hbm, msg, prod_hbm, stage, feats, taps, decay, prod, shifts, lengths, sems
-):
-    _, tokens, channels = feats.shape
+def product_of(shifts, feats, taps):
+    first, third = (short_conv(shifts, f, t) for f, t in zip(feats, taps))
+    product = first.astype(jnp.float32) * third.astype(jnp.float32)
+    inside = rows_of(product.shape) >= HEAD
+    return jnp.where(inside, product, 0.0).astype(jnp.bfloat16)
+
+
+def front_body(lengths_hbm, here, feats_hbm, taps_hbm, decay_hbm, msg, stage, feats, tail, taps, decay, shifts, lengths, sems):
+    pair, tokens, channels = feats.shape
     modes = decay.shape[0]
     groups = channels // LANES
-    wide = 2 * LANES
-    count = channels // wide
-
-    def fetched(block):
-        lanes = slice(block * wide, (block + 1) * wide)
-        return pltpu.make_async_copy(feats_hbm.at[:, :, lanes], feats.at[:, :, lanes], sems.at[3 + block])
-
-    def stored(block):
-        lanes = slice(block * wide, (block + 1) * wide)
-        return pltpu.make_async_copy(prod.at[:, lanes], prod_hbm.at[:, lanes], sems.at[3 + count + block])
-
     counted = pltpu.make_async_copy(lengths_hbm, lengths, sems.at[0])
-    others = (
-        pltpu.make_async_copy(taps_hbm, taps, sems.at[1]),
-        pltpu.make_async_copy(decay_hbm, decay, sems.at[2]),
-    )
+    others = [
+        pltpu.make_async_copy(feats_hbm.at[2 * k], feats.at[k], sems.at[1 + k]) for k in range(pair)
+    ] + [
+        pltpu.make_async_copy(taps_hbm, taps, sems.at[3]),
+        pltpu.make_async_copy(decay_hbm, decay, sems.at[4]),
+        pltpu.make_async_copy(feats_hbm.at[1, tokens - 2 * SUB : tokens, :], tail, sems.at[5]),
+    ]
     counted.start()
-    fetched(0).start()
     for copy in others:
         copy.start()
-    for block in range(1, count):
-        fetched(block).start()
     states = groups * modes
     used = states + 5 * HEAD * groups
     if used < stage.shape[0]:
@@ -93,55 +87,47 @@
     fill_shifts(shifts, lengths, here[0] * tokens)
     for copy in others:
         copy.wait()
-    for block in range(count):
-        lanes = slice(block * wide, (block + 1) * wide)
-        fetched(block).wait()
-        first, third = (
-            short_conv(shifts[...], feats[b, :, lanes], lambda i, b=b: taps[b, i : i + 1, lanes])
-            for b in (0, 2)
-        )
-        product = first.astype(jnp.float32) * third.astype(jnp.float32)
-        product = jnp.where(rows_of((tokens, wide)) >= HEAD, product, 0.0).astype(jnp.bfloat16)
-        prod[:, lanes] = product
-        stored(block).start()
-        values = product.astype(jnp.float32)
-        for half in range(wide // LANES):
-            j = block * (wide // LANES) + half
-            mine = slice(j * LANES, (j + 1) * LANES)
-            v = values[:, half * LANES : (half + 1) * LANES]
-            tables = powers(jnp.exp(-decay[:, mine]))
-            for m in range(modes):
-                one, two, four, eight = (spread(t[m : m + 1]) for t in tables)
-                state = v[0:SUB]
-                for q in range(1, tokens // SUB):
-                    state = state * eight + v[q * SUB : (q + 1) * SUB]
-                state = state * four + pltpu.roll(state, SUB - 4, 0)
-                state = state * two + pltpu.roll(state, SUB - 2, 0)
-                state = state * one + pltpu.roll(state, SUB - 1, 0)
-                stage[j * modes + m : j * modes + m + 1, :] = state[0:1]
-            at = states
-            for b, low in ((0, True), (2, True), (1, True), (0, False), (2, False)):
-                part = feats[b, tokens - 2 * SUB : tokens, mine] if low else feats[b, 0 : 2 * SUB, mine]
-                part = part.astype(jnp.float32)
-                skip = 2 * SUB - HEAD if low else 0
-                for r in range(HEAD):
-                    stage[at + r * groups + j : at + r * groups + j + 1, :] = part[skip + r : skip + r + 1]
-                at += HEAD * groups
+    values = product_of(
+        shifts[...],
+        [feats[k] for k in range(pair)],
+        [lambda i, k=k: taps[2 * k, i : i + 1, :] for k in range(pair)],
+    ).astype(jnp.float32)
+    for j in range(groups):
+        mine = slice(j * LANES, (j + 1) * LANES)
+        v = values[:, mine]
+        tables = powers(jnp.exp(-decay[:, mine]))
+        for m in range(modes):
+            one, two, four, eight = (spread(t[m : m + 1]) for t in tables)
+            state = v[0:SUB]
+            for q in range(1, tokens // SUB):
+                state = state * eight + v[q * SUB : (q + 1) * SUB]
+            state = state * four + pltpu.roll(state, SUB - 4, 0)
+            state = state * two + pltpu.roll(state, SUB - 2, 0)
+            state = state * one + pltpu.roll(state, SUB - 1, 0)
+            stage[j * modes + m : j * modes + m + 1, :] = state[0:1]
+        at = states
+        last = slice(tokens - 2 * SUB, tokens)
+        for part, skip in (
+            (feats[0, last, mine], 2 * SUB - HEAD),
+            (feats[1, last, mine], 2 * SUB - HEAD),
+            (tail[:, mine], 2 * SUB - HEAD),
+            (feats[0, 0 : 2 * SUB, mine], 0),
+            (feats[1, 0 : 2 * SUB, mine], 0),
+        ):
+            part = part.astype(jnp.float32)
+            for r in range(HEAD):
+                stage[at + r * groups + j : at + r * groups + j + 1, :] = part[skip + r : skip + r + 1]
+            at += HEAD * groups
     for c in range(stage.shape[0] // LANES):
         msg[:, c * LANES : (c + 1) * LANES] = stage[c * LANES : (c + 1) * LANES, :].T.astype(jnp.bfloat16)
-    for block in range(count):
-        stored(block).wait()
 
 
 def local_body(
-    lengths, here, feats_hbm, prod_hbm, taps, decay, residue, gate, near, edge, owned, table, feats, prod, shifts, sems
+    lengths, here, feats_hbm, taps, decay, residue, gate, near, edge, owned, table, feats, prod, shifts, sems
 ):
-    tokens, channels = feats.shape
+    _, tokens, channels = feats.shape
     modes = decay.shape[0]
-    copies = (
-        pltpu.make_async_copy(feats_hbm.at[1], feats, sems.at[0]),
-        pltpu.make_async_copy(prod_hbm, prod, sems.at[1]),
-    )
+    copies = [pltpu.make_async_copy(feats_hbm.at[b], feats.at[b], sems.at[b]) for b in range(3)]
     for copy in copies:
         copy.start()
     fill_shifts(shifts, lengths, here[0] * tokens)
@@ -149,12 +135,17 @@
         copy.wait()
     groups = channels // LANES
     chunks = tokens // SUB
-    wide = 2 * LANES
+    wide = 4 * LANES
     for block in range(channels // wide):
         lanes = slice(block * wide, (block + 1) * wide)
-        gate[:, lanes] = short_conv(shifts[...], feats[:, lanes], lambda i: taps[1, i : i + 1, lanes])
+        gate[:, lanes] = short_conv(shifts[...], feats[1, :, lanes], lambda i: taps[1, i : i + 1, lanes])
+        prod[:, lanes] = product_of(
+            shifts[...],
+            [feats[b, :, lanes] for b in (0, 2)],
+            [lambda i, b=b: taps[b, i : i + 1, lanes] for b in (0, 2)],
+        )
     states = groups * modes
-    edge[...] = feats[0 : 2 * SUB, :].astype(jnp.float32)[0:SUB]
+    edge[...] = feats[1, 0 : 2 * SUB, :].astype(jnp.float32)[0:SUB]
     chosen = rows_of((modes, LANES), 1) == here[0]
     chosen_taps = rows_of((TAPS, LANES), 1) == here[0]
     for j in range(groups):
@@ -178,11 +169,12 @@
     def group(j, carry):
         mine = pl.ds(pl.multiple_of(j * LANES, LANES), LANES)
         sums = [jnp.zeros((SUB, LANES), jnp.float32) for _ in range(chunks)]
+        rates = decay[:, mine]
+        weights = residue[:, mine] * jnp.sqrt(2.0 * rates)
+        eights = jnp.exp(-SUB * rates)
         for m in range(modes):
-            rate = decay[m : m + 1, mine]
-            weight = residue[m : m + 1, mine] * jnp.sqrt(2.0 * rate)
-            step = jnp.broadcast_to(jnp.exp(-SUB * rate), (SUB, LANES))
-            wave = weight * jnp.exp(-rate * steps)
+            step = spread(eights[m : m + 1])
+            wave = weights[m : m + 1] * jnp.exp(-rates[m : m + 1] * steps)
             for q in range(chunks):
                 sums[q] = sums[q] + wave
                 if q + 1 < chunks:
@@ -328,9 +320,7 @@
             gated[q * SUB : (q + 1) * SUB, mine] = value
             squares[q] = squares[q] + value * value
     summed = jnp.sum(jnp.concatenate(squares, axis=0), axis=1, keepdims=True)
-    row = jnp.broadcast_to(summed, (tokens, LANES)).T[0:1, :]
-    for k in range(energy.shape[0]):
-        energy[k : k + 1, :] = row
+    energy[...] = jnp.broadcast_to(summed, (tokens, LANES)).T[0:1, :]
 
 
 def scale_body(energy, gated, gain, mixed, *, width):
@@ -354,13 +344,13 @@
     return -(-rows // (2 * LANES)) * 2 * LANES
 
 
-def kernel(body, name, kinds, outs, scratch, flops, moved, given="vvvv"):
+def kernel(body, name, kinds, outs, scratch, flops, moved):
     spaces = {"s": pltpu.SMEM, "v": pltpu.VMEM, "h": pltpu.HBM}
     return pl.pallas_call(
         body,
         out_shape=outs,
         in_specs=[pl.BlockSpec(memory_space=spaces[k]) for k in kinds],
-        out_specs=tuple(pl.BlockSpec(memory_space=spaces[k]) for k, _ in zip(given, outs)),
+        out_specs=tuple(pl.BlockSpec(memory_space=pltpu.VMEM) for _ in outs),
         scratch_shapes=scratch,
         compiler_params=pltpu.CompilerParams(vmem_limit_bytes=VMEM_LIMIT),
         cost_estimate=pl.CostEstimate(flops=flops, bytes_accessed=moved, transcendentals=0),
@@ -384,28 +374,27 @@
         front_body,
         "front",
         "hshhh",
-        (sds((blocks, out_rows), bf16), sds((tokens, channels), bf16)),
+        (sds((blocks, out_rows), bf16),),
         [
             vmem((out_rows, LANES), f32),
-            vmem(features.shape, bf16),
+            vmem((2, tokens, channels), bf16),
+            vmem((2 * SUB, channels), bf16),
             vmem(short_taps.shape, f32),
             vmem(decay.shape, f32),
-            vmem((tokens, channels), bf16),
             vmem((HEAD * tokens, tokens), bf16),
             pltpu.SMEM(doc_lengths.shape, jnp.int32),
-            pltpu.SemaphoreType.DMA((3 + 2 * (channels // (2 * LANES)),)),
+            pltpu.SemaphoreType.DMA((6,)),
         ],
         10**7,
         4 * 10**6,
-        "vh",
     )
     far = functools.partial(pltpu.with_memory_space_constraint, memory_space=pltpu.HBM)
-    msg, prod = front(far(doc_lengths), here, far(features), far(short_taps), far(decay))
+    msg = front(far(doc_lengths), here, far(features), far(short_taps), far(decay))[0]
     arrived = exchange(msg)
     local = kernel(
         local_body,
         "local",
-        "sshhvvv",
+        "sshvvv",
         (
             sds((tokens, channels), bf16),
             sds((tokens, channels), f32),
@@ -414,15 +403,15 @@
         ),
         [
             vmem((tokens, LANES), f32),
-            vmem((tokens, channels), bf16),
+            vmem(features.shape, bf16),
             vmem((tokens, channels), bf16),
             vmem((HEAD * tokens, tokens), bf16),
-            pltpu.SemaphoreType.DMA((2,)),
+            pltpu.SemaphoreType.DMA((3,)),
         ],
         10**8,
         8 * 10**6,
     )
-    gate, near, edge, owned = local(doc_lengths, here, far(features), far(prod), short_taps, decay, residue)
+    gate, near, edge, owned = local(doc_lengths, here, far(features), short_taps, decay, residue)
     owner = kernel(
         functools.partial(owner_body, tokens=tokens, modes=modes),
         "owner",
@@ -438,13 +427,13 @@
         join_body,
         "join",
         "ssvvvvvvv",
-        (sds((tokens, channels), f32), sds((parts, tokens), f32)),
+        (sds((tokens, channels), f32), sds((1, tokens), f32)),
         [vmem((back_rows, LANES), f32)],
         10**7,
         5 * 10**6,
     )
     gated, energy = join(doc_lengths, here, given, near, gate, edge, decay, residue, short_taps)
-    energy = lax.all_to_all(energy.reshape(parts, 1, tokens), "ch", split_axis=0, concat_axis=0, tiled=True)
+    energy = lax.all_gather(energy, "ch", tiled=True)
     scale = kernel(
         functools.partial(scale_body, width=float(channels * parts)),
         "scale",
@@ -454,7 +443,7 @@
         10**6,
         2 * 10**6,
     )
-    return scale(energy.reshape(parts, tokens), gated, gain.reshape(1, channels))[0]
+    return scale(energy, gated, gain.reshape(1, channels))[0]
 
 
 def solution(mesh):

time: 95.3 us -> 89.4 us (0.938)
  blocking collectives: 44.7 us -> 40.3 us
  waiting for transfers between devices: 7.45 us -> 5.88 us
    all_to_all x1 -> x0, blocking collectives: 21.8 us -> none  [per_device(): lax.all_to_all(energy.reshape(parts, 1, tokens), 'ch', split_axis=0, conc...]
    all_gather x0 -> x1, blocking collectives: none -> 16.3 us  [per_device(): energy = lax.all_gather(energy, 'ch', tiled=True)]
    all_to_all x1, waiting for transfers between devices: 7.45 us -> 5.88 us  [exchange(): lax.all_to_all(block.reshape(blocks, 2, width // 2), ('gr', 'gc'), split_...]
    all_to_all x1, blocking collectives: 22.8 us -> 24 us  [exchange(): lax.all_to_all(block.reshape(blocks, 2, width // 2), ('gr', 'gc'), split_...]
  transfers between devices with their start and end apart: 1 -> 1, of which waited for: 1 -> 1; matrix products, arithmetic and copies ran while one was open for 0% -> 0% of each run, Pallas kernels for 10% -> 13%
where the time goes in v4:
time: 89.4 us; the launch traced here: 89.1 us
  blocking collectives  40.3 us (45%)
  Pallas kernels  21.6 us (24%)
  starting transfers between devices  20.4 us (23%)
  waiting for transfers between devices  5.88 us (7%)
    all_to_all x1, blocking collectives, exchange(): lax.all_to_all(block.reshape(blocks, 2, width // 2), ('gr', 'gc'), split_...  24 us
    all_to_all x1, starting transfers between devices, exchange(): lax.all_to_all(block.reshape(blocks, 2, width // 2), ('gr', 'gc'), split_...  20.4 us
    all_gather x1, blocking collectives, per_device(): energy = lax.all_gather(energy, 'ch', tiled=True)  16.3 us
    pallas_call x1, Pallas kernels, per_device(): local(doc_lengths, here, far(features), short_taps, decay, residue)  11.1 us
    all_to_all x1, waiting for transfers between devices, exchange(): lax.all_to_all(block.reshape(blocks, 2, width // 2), ('gr', 'gc'), split_...  5.88 us
    pallas_call x1, Pallas kernels, per_device(): front(far(doc_lengths), here, far(features), far(short_taps), far(decay))[0]  4.93 us
    pallas_call x1, Pallas kernels, per_device(): join(doc_lengths, here, given, near, gate, edge, decay, residue, short_taps)  2.94 us
  transfers between devices with their start and end apart: 1, of which 1 were waited for; matrix products, arithmetic and copies ran while one was open for 0% of the time, Pallas kernels for 13%

profile of v4, /device:TPU:1, one launch (start us, length us, event | category | flops | bytes accessed | tf_op | source)
XLA Modules:
  0.0 89.1 jit_solution(18389077610093638630)
XLA Ops:
  0.0 0.0 copy-start.4
  0.0 0.0 copy-start.1
  0.0 0.0 copy-start
  0.0 0.0 copy-start.2
  0.0 4.9 %front.1 = bf16[128,768]{1,0:T(8,128)(2,1)S(1)} custom-call(s32[8]{0:T(128)} %lengths.5, s32[1]{0:T(128)} %bitcast.here, bf16[3,128,2048]{2,1,0:T(8,128)(2,1)} %feats_hbm.3, f32[3,7,2048]{2,1,0:T(8,128)} %taps.3, f32[16,2048]{1,0:T(8,128)} %decay.3), custom_call_target="tpu_custom_call" | custom-call | flops 10000000 | bytes 4000000 | tf_op jit(solution)/shard_map/front/pallas_call | solution.py:392
  5.0 0.7 reshape.19
  5.7 20.4 %all-to-all-start = ((bf16[128,2,384]{2,1,0:T(2,128)(2,1)}), bf16[128,2,384]{2,1,0:T(2,128)(2,1)S(1)}, u32[]{:S(2)}, u32[]{:S(2)}) async-start(bf16[128,2,384]{2,1,0:T(2,128)(2,1)} %reshape.19), calls=%async_computation | async-start | bytes 393216 | tf_op jit(solution)/shard_map/all_to_all | solution.py:337
  26.1 0.0 copy-done.4
  26.1 0.0 copy-done.1
  26.1 0.0 copy-done
  26.1 0.0 copy-done.2
  26.1 11.1 %local.1 = (bf16[128,2048]{1,0:T(8,128)(2,1)S(1)}, f32[128,2048]{1,0:T(8,128)S(1)}, f32[8,2048]{1,0:T(8,128)S(1)}, f32[848,128]{1,0:T(8,128)S(1)}) custom-call(s32[8]{0:T(128)S(1)} %copy-done.4, s32[1]{0:T(128)} %bitcast.here, bf16[3,128,2048]{2,1,0:T(8,128)(2,1)} %feats_hbm.3, f32[3,7,2048]{2,1,0:T(8,128)S(1)} %copy-done, f32[16,2048]{1,0:T(8,128)S(1)} %copy-done.1, ...), custom_call_target="tpu_custom_call" | custom-call | flops 100000000 | bytes 8000000 | tf_op jit(solution)/shard_map/local/pallas_call | solution.py:414
  37.3 5.9 %all-to-all-done = bf16[128,2,384]{2,1,0:T(2,128)(2,1)S(1)} async-done(((bf16[128,2,384]{2,1,0:T(2,128)(2,1)}), bf16[128,2,384]{2,1,0:T(2,128)(2,1)S(1)}, u32[]{:S(2)}, u32[]{:S(2)}) %all-to-all-start) | async-done | bytes 196640 | tf_op jit(solution)/shard_map/all_to_all | solution.py:337
  43.2 1.6 %owner.1 = bf16[128,512]{1,0:T(8,128)(2,1)S(1)} custom-call(s32[8]{0:T(128)S(1)} %copy-done.4, bf16[128,768]{1,0:T(8,128)(2,1)S(1)} %bitcast.8, f32[848,128]{1,0:T(8,128)S(1)} %get-tuple-element.11.owned), custom_call_target="tpu_custom_call" | custom-call | flops 1000000 | bytes 1000000 | tf_op jit(solution)/shard_map/owner/pallas_call | solution.py:424
  44.8 0.0 copy-start.3
  44.9 24.0 %all_to_all.10 = bf16[128,2,256]{2,1,0:T(2,128)(2,1)S(1)} all-to-all(bf16[128,2,256]{2,1,0:T(2,128)(2,1)S(1)} %reshape.21), channel_id=1, replica_groups=mesh['ch'=4,'gr'=16,'gc'=8] {'gr','gc'}, dimensions={0} | all-to-all | bytes 262144 | tf_op jit(solution)/shard_map/all_to_all | solution.py:337
  68.9 2.9 %join.1 = (f32[128,2048]{1,0:T(8,128)S(1)}, f32[1,128]{1,0:T(1,128)S(1)}) custom-call(s32[8]{0:T(128)S(1)} %copy-done.4, s32[1]{0:T(128)} %bitcast.here, bf16[128,512]{1,0:T(8,128)(2,1)S(1)} %bitcast.9, f32[128,2048]{1,0:T(8,128)S(1)} %get-tuple-element.12.near, bf16[128,2048]{1,0:T(8,128)(2,1)S(1)} %get-tuple-element.13.gate, ...), custom_call_target="tpu_custom_call" | custom-call | flops 10000000 | bytes 5000000 | tf_op jit(solution)/shard_map/join/pallas_call | solution.py:435
  71.8 16.3 %all-gather = f32[4,1,128]{2,1,0:T(1,128)S(1)} all-gather(f32[1,1,128]{2,1,0:T(1,128)S(1)} %bitcast.12), channel_id=1, replica_groups=mesh['ch'=4,'gr'=16,'gc'=8] {'ch'}, dimensions={0}, use_global_device_ids=true | all-gather | bytes 2560 | tf_op jit(solution)/shard_map/all_gather | solution.py:436
  88.1 0.0 copy-done.3
  88.1 1.0 %scale.1 = bf16[128,2048]{1,0:T(8,128)(2,1)} custom-call(f32[4,128]{1,0:T(4,128)S(1)} %bitcast.11, f32[128,2048]{1,0:T(8,128)S(1)} %get-tuple-element.16.gated, f32[1,2048]{1,0:T(1,128)S(1)} %bitcast.10), custom_call_target="tpu_custom_call" | custom-call | flops 1000000 | bytes 2000000 | tf_op jit(solution)/shard_map/scale/pallas_call | solution.py:446
  (3 shorter events, 0.1 us)
Async XLA Ops:
  0.0 26.1 %copy-start.4 = (s32[8]{0:T(128)S(1)}, s32[8]{0:T(128)}, u32[]{:S(2)}) copy-start(s32[8]{0:T(128)} %lengths.5) | copy-start | bytes 100
  0.0 26.1 %copy-start.1 = (f32[16,2048]{1,0:T(8,128)S(1)}, f32[16,2048]{1,0:T(8,128)}, u32[]{:S(2)}) copy-start(f32[16,2048]{1,0:T(8,128)} %decay.3) | copy-start | bytes 393220
  0.0 26.1 %copy-start = (f32[3,7,2048]{2,1,0:T(8,128)S(1)}, f32[3,7,2048]{2,1,0:T(8,128)}, u32[]{:S(2)}) copy-start(f32[3,7,2048]{2,1,0:T(8,128)} %taps.3) | copy-start | bytes 516100
  0.0 26.1 %copy-start.2 = (f32[16,2048]{1,0:T(8,128)S(1)}, f32[16,2048]{1,0:T(8,128)}, u32[]{:S(2)}) copy-start(f32[16,2048]{1,0:T(8,128)} %residue.3) | copy-start | bytes 393220
  5.7 37.5 %all-to-all-start = ((bf16[128,2,384]{2,1,0:T(2,128)(2,1)}), bf16[128,2,384]{2,1,0:T(2,128)(2,1)S(1)}, u32[]{:S(2)}, u32[]{:S(2)}) async-start(bf16[128,2,384]{2,1,0:T(2,128)(2,1)} %reshape.19), calls=%async_computation | async-start | bytes 393216 | tf_op jit(solution)/shard_map/all_to_all | solution.py:337
  44.8 43.3 %copy-start.3 = (f32[2048]{0:T(1024)S(1)}, f32[2048]{0:T(1024)}, u32[]{:S(2)}) copy-start(f32[2048]{0:T(1024)} %param.11) | copy-start | bytes 24580

commit v5 on v4

--- a/solution.py
+++ b/solution.py
@@ -57,11 +57,9 @@
         shifts[(i - 1) * tokens : i * tokens, :] = jnp.where(hit, 1.0, 0.0).astype(jnp.bfloat16)
 
 
-def product_of(shifts, feats, taps):
-    first, third = (short_conv(shifts, f, t) for f, t in zip(feats, taps))
+def product_of(first, third):
     product = first.astype(jnp.float32) * third.astype(jnp.float32)
-    inside = rows_of(product.shape) >= HEAD
-    return jnp.where(inside, product, 0.0).astype(jnp.bfloat16)
+    return jnp.where(rows_of(product.shape) >= HEAD, product, 0.0).astype(jnp.bfloat16)
 
 
 def front_body(lengths_hbm, here, feats_hbm, taps_hbm, decay_hbm, msg, stage, feats, tail, taps, decay, shifts, lengths, sems):
@@ -69,14 +67,16 @@
     modes = decay.shape[0]
     groups = channels // LANES
     counted = pltpu.make_async_copy(lengths_hbm, lengths, sems.at[0])
-    others = [
-        pltpu.make_async_copy(feats_hbm.at[2 * k], feats.at[k], sems.at[1 + k]) for k in range(pair)
-    ] + [
-        pltpu.make_async_copy(taps_hbm, taps, sems.at[3]),
+    branches = [pltpu.make_async_copy(feats_hbm.at[2 * k], feats.at[k], sems.at[1 + k]) for k in range(pair)]
+    tapped = pltpu.make_async_copy(taps_hbm, taps, sems.at[3])
+    others = (
         pltpu.make_async_copy(decay_hbm, decay, sems.at[4]),
         pltpu.make_async_copy(feats_hbm.at[1, tokens - 2 * SUB : tokens, :], tail, sems.at[5]),
-    ]
+    )
     counted.start()
+    branches[0].start()
+    tapped.start()
+    branches[1].start()
     for copy in others:
         copy.start()
     states = groups * modes
@@ -85,13 +85,14 @@
         stage[used:, :] = jnp.zeros((stage.shape[0] - used, LANES), jnp.float32)
     counted.wait()
     fill_shifts(shifts, lengths, here[0] * tokens)
+    tapped.wait()
+    found = []
+    for k in range(pair):
+        branches[k].wait()
+        found.append(short_conv(shifts[...], feats[k], lambda i, k=k: taps[2 * k, i : i + 1, :]))
+    values = product_of(*found).astype(jnp.float32)
     for copy in others:
         copy.wait()
-    values = product_of(
-        shifts[...],
-        [feats[k] for k in range(pair)],
-        [lambda i, k=k: taps[2 * k, i : i + 1, :] for k in range(pair)],
-    ).astype(jnp.float32)
     for j in range(groups):
         mine = slice(j * LANES, (j + 1) * LANES)
         v = values[:, mine]
@@ -140,9 +141,10 @@
         lanes = slice(block * wide, (block + 1) * wide)
         gate[:, lanes] = short_conv(shifts[...], feats[1, :, lanes], lambda i: taps[1, i : i + 1, lanes])
         prod[:, lanes] = product_of(
-            shifts[...],
-            [feats[b, :, lanes] for b in (0, 2)],
-            [lambda i, b=b: taps[b, i : i + 1, lanes] for b in (0, 2)],
+            *(
+                short_conv(shifts[...], feats[b, :, lanes], lambda i, b=b: taps[b, i : i + 1, lanes])
+                for b in (0, 2)
+            )
         )
     states = groups * modes
     edge[...] = feats[1, 0 : 2 * SUB, :].astype(jnp.float32)[0:SUB]
@@ -150,18 +152,21 @@
     chosen_taps = rows_of((TAPS, LANES), 1) == here[0]
     for j in range(groups):
         mine = slice(j * LANES, (j + 1) * LANES)
-        at = slice(j * modes, (j + 1) * modes)
         rates, scale = decay[:, mine], residue[:, mine]
         scale = scale * jnp.sqrt(2.0 * rates)
         pick = jnp.sum(jnp.where(chosen, rates, 0.0), axis=1, keepdims=True)
-        owned[at, :] = jnp.broadcast_to(pick, (modes, LANES))
+        pick = jnp.broadcast_to(pick, (modes, LANES))
+        for k, count in enumerate((1, tokens - HEAD, tokens)):
+            to = k * states + j * modes
+            owned[to : to + modes, :] = jnp.exp(-pick * count)
         pick = jnp.sum(jnp.where(chosen, scale, 0.0), axis=1, keepdims=True)
-        owned[states + j * modes : states + (j + 1) * modes, :] = jnp.broadcast_to(pick, (modes, LANES))
+        to = 3 * states + j * modes
+        owned[to : to + modes, :] = jnp.broadcast_to(pick, (modes, LANES))
         for b in range(3):
             pick = jnp.sum(jnp.where(chosen_taps, taps[b, :, mine], 0.0), axis=1, keepdims=True)
             pick = jnp.broadcast_to(pick, (TAPS, LANES))
             for i in range(TAPS):
-                to = 2 * states + (b * TAPS + i) * groups + j
+                to = 4 * states + (b * TAPS + i) * groups + j
                 owned[to : to + 1, :] = pick[i : i + 1]
     inside = rows_of((SUB, LANES))
     steps = inside.astype(jnp.float32)
@@ -207,7 +212,7 @@
 
 def owner_body(lengths, arrived, owned, back, stage, out, *, tokens, modes):
     blocks = arrived.shape[0]
-    groups = owned.shape[0] // (2 * modes + 3 * TAPS)
+    groups = owned.shape[0] // (4 * modes + 3 * TAPS)
     states = modes * groups
     for c in range(stage.shape[0] // LANES):
         stage[c * LANES : (c + 1) * LANES, :] = arrived[:, c * LANES : (c + 1) * LANES].astype(jnp.float32).T
@@ -231,7 +236,7 @@
         for r in range(HEAD):
             total = jnp.zeros((groups, blocks), jnp.float32)
             for i in range(TAPS):
-                at = 2 * states + (b * TAPS + i) * groups
+                at = 4 * states + (b * TAPS + i) * groups
                 term = owned[at : at + groups, :] * ext[HEAD + r - i]
                 total = total + jnp.where(reach[r] >= i, term, 0.0)
             found.append(total.astype(jnp.bfloat16).astype(jnp.float32))
@@ -240,14 +245,14 @@
     lane = rows_of((modes, blocks), 1)
     for j in range(groups):
         at = slice(j * modes, (j + 1) * modes)
-        rate, weight = owned[at, :], owned[states + j * modes : states + (j + 1) * modes, :]
-        ratio = jnp.exp(-rate)
+        ratio, distant, decline, weight = (
+            owned[k * states + j * modes : k * states + (j + 1) * modes, :] for k in range(4)
+        )
         rows = [spread(p[j : j + 1], modes) for p in products]
         head = rows[0]
         for r in range(1, HEAD):
             head = head * ratio + rows[r]
-        total = stage[at, :] + jnp.exp(-rate * (tokens - HEAD)) * head
-        decline = jnp.exp(-rate * tokens)
+        total = stage[at, :] + distant * head
         distance = 1
         while distance < blocks:
             shifted = jnp.where(lane >= distance, pltpu.roll(total, distance, 1), 0.0)
@@ -302,16 +307,14 @@
                 total[q] = total[q] + wave
                 if q + 1 < chunks:
                     wave = wave * eight
-        at = states + j
-        pieces = [stage[at + r * groups : at + r * groups + 1, :] for r in range(HEAD)]
-        total[0] = jnp.concatenate(pieces + [total[0][HEAD:SUB]], axis=0)
-        at += HEAD * groups
-        pieces = [stage[at + r * groups : at + r * groups + 1, :] for r in range(HEAD)]
-        ext = jnp.concatenate(pieces + [edge[:, mine], jnp.zeros((2, LANES), jnp.float32)], axis=0)
-        front = jnp.zeros((SUB, LANES), jnp.float32)
-        for i in range(TAPS):
-            term = taps[1, i : i + 1, mine] * ext[HEAD - i : HEAD - i + SUB]
-            front = front + jnp.where(reach >= i, term, 0.0)
+        told = stage[pl.ds(states + j, SUB, stride=groups), :]
+        total[0] = jnp.where(inside < HEAD, told, total[0])
+        before = stage[pl.ds(states + HEAD * groups + j, SUB, stride=groups), :]
+        now = edge[:, mine]
+        front = now * taps[1, 0:1, mine]
+        for i in range(1, TAPS):
+            moved = jnp.where(inside < i, pltpu.roll(before, (SUB - HEAD + i) % SUB, 0), pltpu.roll(now, i, 0))
+            front = front + jnp.where(reach >= i, moved * taps[1, i : i + 1, mine], 0.0)
         front = front.astype(jnp.bfloat16).astype(jnp.float32)
         gates = gate[:, mine].astype(jnp.float32)
         for q in range(chunks):
@@ -323,13 +326,22 @@
     energy[...] = jnp.broadcast_to(summed, (tokens, LANES)).T[0:1, :]
 
 
-def scale_body(energy, gated, gain, mixed, *, width):
+def scale_body(energy, gated, gain, mixed_hbm, mixed, sems, *, width):
     tokens, channels = gated.shape
+    pieces = sems.shape[0]
+    rows = tokens // pieces
     scaling = lax.rsqrt(jnp.sum(energy[...], axis=0, keepdims=True) / width + 1e-06)
     scaling = jnp.broadcast_to(scaling, (LANES, tokens)).T
-    for j in range(channels // LANES):
-        mine = slice(j * LANES, (j + 1) * LANES)
-        mixed[:, mine] = (gated[:, mine] * scaling * gain[:, mine]).astype(jnp.bfloat16)
+    copies = []
+    for k in range(pieces):
+        part = slice(k * rows, (k + 1) * rows)
+        for j in range(channels // LANES):
+            mine = slice(j * LANES, (j + 1) * LANES)
+            mixed[part, mine] = (gated[part, mine] * scaling[part] * gain[:, mine]).astype(jnp.bfloat16)
+        copies.append(pltpu.make_async_copy(mixed.at[part, :], mixed_hbm.at[part, :], sems.at[k]))
+        copies[k].start()
+    for copy in copies:
+        copy.wait()
 
 
 def exchange(block):
@@ -344,13 +356,13 @@
     return -(-rows // (2 * LANES)) * 2 * LANES
 
 
-def kernel(body, name, kinds, outs, scratch, flops, moved):
+def kernel(body, name, kinds, outs, scratch, flops, moved, to=pltpu.VMEM):
     spaces = {"s": pltpu.SMEM, "v": pltpu.VMEM, "h": pltpu.HBM}
     return pl.pallas_call(
         body,
         out_shape=outs,
         in_specs=[pl.BlockSpec(memory_space=spaces[k]) for k in kinds],
-        out_specs=tuple(pl.BlockSpec(memory_space=pltpu.VMEM) for _ in outs),
+        out_specs=tuple(pl.BlockSpec(memory_space=to) for _ in outs),
         scratch_shapes=scratch,
         compiler_params=pltpu.CompilerParams(vmem_limit_bytes=VMEM_LIMIT),
         cost_estimate=pl.CostEstimate(flops=flops, bytes_accessed=moved, transcendentals=0),
@@ -399,7 +411,7 @@
             sds((tokens, channels), bf16),
             sds((tokens, channels), f32),
             sds((SUB, channels), f32),
-            sds((2 * states + 3 * TAPS * groups, LANES), f32),
+            sds((4 * states + 3 * TAPS * groups, LANES), f32),
         ),
         [
             vmem((tokens, LANES), f32),
@@ -439,9 +451,10 @@
         "scale",
         "vvv",
         (sds((tokens, channels), bf16),),
-        [],
+        [vmem((tokens, channels), bf16), pltpu.SemaphoreType.DMA((4,))],
         10**6,
         2 * 10**6,
+        pltpu.HBM,
     )
     return scale(energy, gated, gain.reshape(1, channels))[0]
 

time: 89.4 us -> 89.5 us (level)
  no operation moved by 1% of the time
where the time goes in v5:
time: 89.5 us; the launch traced here: 89.2 us
  blocking collectives  40.3 us (45%)
  Pallas kernels  21.6 us (24%)
  starting transfers between devices  20.4 us (23%)
  waiting for transfers between devices  5.85 us (7%)
    all_to_all x1, blocking collectives, exchange(): lax.all_to_all(block.reshape(blocks, 2, width // 2), ('gr', 'gc'), split_...  24 us
    all_to_all x1, starting transfers between devices, exchange(): lax.all_to_all(block.reshape(blocks, 2, width // 2), ('gr', 'gc'), split_...  20.4 us
    all_gather x1, blocking collectives, per_device(): energy = lax.all_gather(energy, 'ch', tiled=True)  16.3 us
    pallas_call x1, Pallas kernels, per_device(): local(doc_lengths, here, far(features), short_taps, decay, residue)  11.2 us
    all_to_all x1, waiting for transfers between devices, exchange(): lax.all_to_all(block.reshape(blocks, 2, width // 2), ('gr', 'gc'), split_...  5.85 us
    pallas_call x1, Pallas kernels, per_device(): front(far(doc_lengths), here, far(features), far(short_taps), far(decay))[0]  4.97 us
    pallas_call x1, Pallas kernels, per_device(): join(doc_lengths, here, given, near, gate, edge, decay, residue, short_taps)  2.89 us
  transfers between devices with their start and end apart: 1, of which 1 were waited for; matrix products, arithmetic and copies ran while one was open for 0% of the time, Pallas kernels for 13%

profile of v5, /device:TPU:1, one launch (start us, length us, event | category | flops | bytes accessed | tf_op | source)
XLA Modules:
  0.0 89.2 jit_solution(10421062196792053664)
XLA Ops:
  0.0 0.0 copy-start.4
  0.0 0.0 copy-start.1
  0.0 0.0 copy-start
  0.0 0.0 copy-start.2
  0.0 5.0 %front.1 = bf16[128,768]{1,0:T(8,128)(2,1)S(1)} custom-call(s32[8]{0:T(128)} %lengths.5, s32[1]{0:T(128)} %bitcast.here, bf16[3,128,2048]{2,1,0:T(8,128)(2,1)} %feats_hbm.3, f32[3,7,2048]{2,1,0:T(8,128)} %taps.3, f32[16,2048]{1,0:T(8,128)} %decay.3), custom_call_target="tpu_custom_call" | custom-call | flops 10000000 | bytes 4000000 | tf_op jit(solution)/shard_map/front/pallas_call | solution.py:404
  5.0 0.7 reshape.19
  5.7 20.4 %all-to-all-start = ((bf16[128,2,384]{2,1,0:T(2,128)(2,1)}), bf16[128,2,384]{2,1,0:T(2,128)(2,1)S(1)}, u32[]{:S(2)}, u32[]{:S(2)}) async-start(bf16[128,2,384]{2,1,0:T(2,128)(2,1)} %reshape.19), calls=%async_computation | async-start | bytes 393216 | tf_op jit(solution)/shard_map/all_to_all | solution.py:349
  26.1 0.0 copy-done.4
  26.1 0.0 copy-done.1
  26.2 0.0 copy-done
  26.2 0.0 copy-done.2
  26.2 11.2 %local.1 = (bf16[128,2048]{1,0:T(8,128)(2,1)S(1)}, f32[128,2048]{1,0:T(8,128)S(1)}, f32[8,2048]{1,0:T(8,128)S(1)}, f32[1360,128]{1,0:T(8,128)S(1)}) custom-call(s32[8]{0:T(128)S(1)} %copy-done.4, s32[1]{0:T(128)} %bitcast.here, bf16[3,128,2048]{2,1,0:T(8,128)(2,1)} %feats_hbm.3, f32[3,7,2048]{2,1,0:T(8,128)S(1)} %copy-done, f32[16,2048]{1,0:T(8,128)S(1)} %copy-done.1, ...), custom_call_target="tpu_custom_call" | custom-call | flops 100000000 | bytes 8000000 | tf_op jit(solution)/shard_map/local/pallas_call | solution.py:426
  37.4 5.8 %all-to-all-done = bf16[128,2,384]{2,1,0:T(2,128)(2,1)S(1)} async-done(((bf16[128,2,384]{2,1,0:T(2,128)(2,1)}), bf16[128,2,384]{2,1,0:T(2,128)(2,1)S(1)}, u32[]{:S(2)}, u32[]{:S(2)}) %all-to-all-start) | async-done | bytes 196640 | tf_op jit(solution)/shard_map/all_to_all | solution.py:349
  43.2 1.6 %owner.1 = bf16[128,512]{1,0:T(8,128)(2,1)S(1)} custom-call(s32[8]{0:T(128)S(1)} %copy-done.4, bf16[128,768]{1,0:T(8,128)(2,1)S(1)} %bitcast.8, f32[1360,128]{1,0:T(8,128)S(1)} %get-tuple-element.11.owned), custom_call_target="tpu_custom_call" | custom-call | flops 1000000 | bytes 1000000 | tf_op jit(solution)/shard_map/owner/pallas_call | solution.py:436
  44.9 0.0 copy-start.3
  44.9 24.0 %all_to_all.10 = bf16[128,2,256]{2,1,0:T(2,128)(2,1)S(1)} all-to-all(bf16[128,2,256]{2,1,0:T(2,128)(2,1)S(1)} %reshape.21), channel_id=1, replica_groups=mesh['ch'=4,'gr'=16,'gc'=8] {'gr','gc'}, dimensions={0} | all-to-all | bytes 262144 | tf_op jit(solution)/shard_map/all_to_all | solution.py:349
  69.0 2.9 %join.1 = (f32[128,2048]{1,0:T(8,128)S(1)}, f32[1,128]{1,0:T(1,128)S(1)}) custom-call(s32[8]{0:T(128)S(1)} %copy-done.4, s32[1]{0:T(128)} %bitcast.here, bf16[128,512]{1,0:T(8,128)(2,1)S(1)} %bitcast.9, f32[128,2048]{1,0:T(8,128)S(1)} %get-tuple-element.12.near, bf16[128,2048]{1,0:T(8,128)(2,1)S(1)} %get-tuple-element.13.gate, ...), custom_call_target="tpu_custom_call" | custom-call | flops 10000000 | bytes 5000000 | tf_op jit(solution)/shard_map/join/pallas_call | solution.py:447
  71.8 16.3 %all-gather = f32[4,1,128]{2,1,0:T(1,128)S(1)} all-gather(f32[1,1,128]{2,1,0:T(1,128)S(1)} %bitcast.12), channel_id=1, replica_groups=mesh['ch'=4,'gr'=16,'gc'=8] {'ch'}, dimensions={0}, use_global_device_ids=true | all-gather | bytes 2560 | tf_op jit(solution)/shard_map/all_gather | solution.py:448
  88.1 0.0 copy-done.3
  88.1 0.9 %scale.1 = bf16[128,2048]{1,0:T(8,128)(2,1)} custom-call(f32[4,128]{1,0:T(4,128)S(1)} %bitcast.11, f32[128,2048]{1,0:T(8,128)S(1)} %get-tuple-element.16.gated, f32[1,2048]{1,0:T(1,128)S(1)} %bitcast.10), custom_call_target="tpu_custom_call" | custom-call | flops 1000000 | bytes 2000000 | tf_op jit(solution)/shard_map/scale/pallas_call | solution.py:459
  (3 shorter events, 0.1 us)
Async XLA Ops:
  0.0 26.1 %copy-start.4 = (s32[8]{0:T(128)S(1)}, s32[8]{0:T(128)}, u32[]{:S(2)}) copy-start(s32[8]{0:T(128)} %lengths.5) | copy-start | bytes 100
  0.0 26.1 %copy-start.1 = (f32[16,2048]{1,0:T(8,128)S(1)}, f32[16,2048]{1,0:T(8,128)}, u32[]{:S(2)}) copy-start(f32[16,2048]{1,0:T(8,128)} %decay.3) | copy-start | bytes 393220
  0.0 26.1 %copy-start = (f32[3,7,2048]{2,1,0:T(8,128)S(1)}, f32[3,7,2048]{2,1,0:T(8,128)}, u32[]{:S(2)}) copy-start(f32[3,7,2048]{2,1,0:T(8,128)} %taps.3) | copy-start | bytes 516100
  0.0 26.2 %copy-start.2 = (f32[16,2048]{1,0:T(8,128)S(1)}, f32[16,2048]{1,0:T(8,128)}, u32[]{:S(2)}) copy-start(f32[16,2048]{1,0:T(8,128)} %residue.3) | copy-start | bytes 393220
  5.7 37.5 %all-to-all-start = ((bf16[128,2,384]{2,1,0:T(2,128)(2,1)}), bf16[128,2,384]{2,1,0:T(2,128)(2,1)S(1)}, u32[]{:S(2)}, u32[]{:S(2)}) async-start(bf16[128,2,384]{2,1,0:T(2,128)(2,1)} %reshape.19), calls=%async_computation | async-start | bytes 393216 | tf_op jit(solution)/shard_map/all_to_all | solution.py:349
  44.9 43.3 %copy-start.3 = (f32[2048]{0:T(1024)S(1)}, f32[2048]{0:T(1024)}, u32[]{:S(2)}) copy-start(f32[2048]{0:T(1024)} %param.11) | copy-start | bytes 24580

commit v6 on v5

--- a/solution.py
+++ b/solution.py
@@ -124,7 +124,7 @@
 
 
 def local_body(
-    lengths, here, feats_hbm, taps, decay, residue, gate, near, edge, owned, table, feats, prod, shifts, sems
+    lengths, here, lane, feats_hbm, taps, decay, residue, gate, near, edge, owned, table, feats, prod, shifts, sems
 ):
     _, tokens, channels = feats.shape
     modes = decay.shape[0]
@@ -148,8 +148,8 @@
         )
     states = groups * modes
     edge[...] = feats[1, 0 : 2 * SUB, :].astype(jnp.float32)[0:SUB]
-    chosen = rows_of((modes, LANES), 1) == here[0]
-    chosen_taps = rows_of((TAPS, LANES), 1) == here[0]
+    chosen = rows_of((modes, LANES), 1) == lane[0]
+    chosen_taps = rows_of((TAPS, LANES), 1) == lane[0]
     for j in range(groups):
         mine = slice(j * LANES, (j + 1) * LANES)
         rates, scale = decay[:, mine], residue[:, mine]
@@ -344,11 +344,17 @@
         copy.wait()
 
 
-def exchange(block):
+def exchange(block, outward):
     blocks, width = block.shape
+    slow, fast = lax.axis_size("gr"), lax.axis_size("gc")
+    half = width // 2
+    if not outward:
+        block = block.reshape(slow, fast, 2, half).transpose(1, 0, 2, 3)
     moved = lax.all_to_all(
-        block.reshape(blocks, 2, width // 2), ("gr", "gc"), split_axis=0, concat_axis=0, tiled=True
-    )
+        block.reshape(blocks, 2, half), ("gc", "gr"), split_axis=0, concat_axis=0, tiled=True
+    )
+    if outward:
+        moved = moved.reshape(fast, slow, 2, half).transpose(1, 0, 2, 3)
     return moved.reshape(blocks, width)
 
 
@@ -377,6 +383,7 @@
     groups = channels // LANES
     states = groups * modes
     here = lax.axis_index(("gr", "gc")).astype(jnp.int32).reshape(1)
+    lane = lax.axis_index(("gc", "gr")).astype(jnp.int32).reshape(1)
     f32, bf16 = jnp.float32, jnp.bfloat16
     sds = jax.ShapeDtypeStruct
     vmem = pltpu.VMEM
@@ -402,11 +409,11 @@
     )
     far = functools.partial(pltpu.with_memory_space_constraint, memory_space=pltpu.HBM)
     msg = front(far(doc_lengths), here, far(features), far(short_taps), far(decay))[0]
-    arrived = exchange(msg)
+    arrived = exchange(msg, True)
     local = kernel(
         local_body,
         "local",
-        "sshvvv",
+        "ssshvvv",
         (
             sds((tokens, channels), bf16),
             sds((tokens, channels), f32),
@@ -423,7 +430,7 @@
         10**8,
         8 * 10**6,
     )
-    gate, near, edge, owned = local(doc_lengths, here, far(features), short_taps, decay, residue)
+    gate, near, edge, owned = local(doc_lengths, here, lane, far(features), short_taps, decay, residue)
     owner = kernel(
         functools.partial(owner_body, tokens=tokens, modes=modes),
         "owner",
@@ -433,7 +440,7 @@
         10**6,
         10**6,
     )
-    given = exchange(owner(doc_lengths, arrived, owned)[0])
+    given = exchange(owner(doc_lengths, arrived, owned)[0], False)
     parts = lax.axis_size("ch")
     join = kernel(
         join_body,

time: 89.5 us -> 90 us (level)
  blocking collectives: 40.3 us -> 43.2 us
  waiting for transfers between devices: 5.85 us -> 3.35 us
    all_to_all x1, waiting for transfers between devices: 5.85 us -> 3.35 us  [exchange(): lax.all_to_all(block.reshape(blocks, 2, half), ('gc', 'gr'), split_axis=0...]
    all_to_all x1, blocking collectives: 24 us -> 26.4 us  [exchange(): lax.all_to_all(block.reshape(blocks, 2, half), ('gc', 'gr'), split_axis=0...]
  transfers between devices with their start and end apart: 1 -> 1, of which waited for: 1 -> 1; matrix products, arithmetic and copies ran while one was open for 0% -> 0% of each run, Pallas kernels for 13% -> 12%
where the time goes in v6:
time: 90 us; the launch traced here: 89.7 us
  blocking collectives  43.2 us (48%)
  Pallas kernels  21.6 us (24%)
  starting transfers between devices  20.4 us (23%)
  waiting for transfers between devices  3.35 us (4%)
  local copies, waits for them, and re-layouts  0.93 us (1%)
    all_to_all x1, blocking collectives, exchange(): lax.all_to_all(block.reshape(blocks, 2, half), ('gc', 'gr'), split_axis=0...  26.4 us
    all_to_all x1, starting transfers between devices, exchange(): lax.all_to_all(block.reshape(blocks, 2, half), ('gc', 'gr'), split_axis=0...  20.4 us
    all_gather x1, blocking collectives, per_device(): energy = lax.all_gather(energy, 'ch', tiled=True)  16.8 us
    pallas_call x1, Pallas kernels, per_device(): local(doc_lengths, here, lane, far(features), short_taps, decay, residue)  11.2 us
    pallas_call x1, Pallas kernels, per_device(): front(far(doc_lengths), here, far(features), far(short_taps), far(decay))[0]  4.97 us
    all_to_all x1, waiting for transfers between devices, exchange(): lax.all_to_all(block.reshape(blocks, 2, half), ('gc', 'gr'), split_axis=0...  3.35 us
    pallas_call x1, Pallas kernels, per_device(): join(doc_lengths, here, given, near, gate, edge, decay, residue, short_taps)  2.89 us
  transfers between devices with their start and end apart: 1, of which 1 were waited for; matrix products, arithmetic and copies ran while one was open for 0% of the time, Pallas kernels for 12%

profile of v6, /device:TPU:1, one launch (start us, length us, event | category | flops | bytes accessed | tf_op | source)
XLA Modules:
  0.0 89.7 jit_solution(6763265819452092060)
XLA Ops:
  0.0 0.0 copy-start.4
  0.0 0.0 copy-start.1
  0.0 0.0 copy-start
  0.0 0.0 copy-start.2
  0.0 5.0 %front.1 = bf16[128,768]{1,0:T(8,128)(2,1)S(1)} custom-call(s32[8]{0:T(128)} %lengths.5, s32[1]{0:T(128)} %bitcast.here, bf16[3,128,2048]{2,1,0:T(8,128)(2,1)} %feats_hbm.3, f32[3,7,2048]{2,1,0:T(8,128)} %taps.3, f32[16,2048]{1,0:T(8,128)} %decay.3), custom_call_target="tpu_custom_call" | custom-call | flops 10000000 | bytes 4000000 | tf_op jit(solution)/shard_map/front/pallas_call | solution.py:411
  5.0 0.7 reshape.28
  5.7 20.4 %all-to-all-start = ((bf16[128,2,384]{2,1,0:T(2,128)(2,1)}), bf16[128,2,384]{2,1,0:T(2,128)(2,1)S(1)}, u32[]{:S(2)}, u32[]{:S(2)}) async-start(bf16[128,2,384]{2,1,0:T(2,128)(2,1)} %reshape.28), calls=%async_computation | async-start | bytes 393216 | tf_op jit(solution)/shard_map/all_to_all | solution.py:353
  26.1 0.0 copy-done.4
  26.1 0.0 copy-done.1
  26.2 0.0 copy-done
  26.2 0.0 copy-done.2
  26.2 11.2 %local.1 = (bf16[128,2048]{1,0:T(8,128)(2,1)S(1)}, f32[128,2048]{1,0:T(8,128)S(1)}, f32[8,2048]{1,0:T(8,128)S(1)}, f32[1360,128]{1,0:T(8,128)S(1)}) custom-call(s32[8]{0:T(128)S(1)} %copy-done.4, s32[1]{0:T(128)} %bitcast.here, s32[1]{0:T(128)} %bitcast.4.lane, bf16[3,128,2048]{2,1,0:T(8,128)(2,1)} %feats_hbm.3, f32[3,7,2048]{2,1,0:T(8,128)S(1)} %copy-done, ...), custom_call_target="tpu_custom_call" | custom-call | flops 100000000 | bytes 8000000 | tf_op jit(solution)/shard_map/local/pallas_call | solution.py:433
  37.4 3.3 %all-to-all-done = bf16[128,2,384]{2,1,0:T(2,128)(2,1)S(1)} async-done(((bf16[128,2,384]{2,1,0:T(2,128)(2,1)}), bf16[128,2,384]{2,1,0:T(2,128)(2,1)S(1)}, u32[]{:S(2)}, u32[]{:S(2)}) %all-to-all-start) | async-done | bytes 196640 | tf_op jit(solution)/shard_map/all_to_all | solution.py:353
  40.8 1.6 %owner.1 = bf16[128,512]{1,0:T(8,128)(2,1)S(1)} custom-call(s32[8]{0:T(128)S(1)} %copy-done.4, bf16[128,768]{1,0:T(8,128)(2,1)S(1)} %bitcast.15, f32[1360,128]{1,0:T(8,128)S(1)} %get-tuple-element.11.owned), custom_call_target="tpu_custom_call" | custom-call | flops 1000000 | bytes 1000000 | tf_op jit(solution)/shard_map/owner/pallas_call | solution.py:443
  42.4 0.0 copy-start.3
  42.4 0.1 copy.15
  42.5 26.4 %all_to_all.10 = bf16[128,2,256]{2,1,0:T(2,128)(2,1)S(1)} all-to-all(bf16[128,2,256]{2,1,0:T(2,128)(2,1)S(1)} %bitcast.22), channel_id=1, replica_groups=mesh['ch'=4,'gr'=16,'gc'=8] {'gc','gr'}, dimensions={0} | all-to-all | bytes 262144 | tf_op jit(solution)/shard_map/all_to_all | solution.py:353
  69.0 2.9 %join.1 = (f32[128,2048]{1,0:T(8,128)S(1)}, f32[1,128]{1,0:T(1,128)S(1)}) custom-call(s32[8]{0:T(128)S(1)} %copy-done.4, s32[1]{0:T(128)} %bitcast.here, bf16[128,512]{1,0:T(8,128)(2,1)S(1)} %bitcast.16, f32[128,2048]{1,0:T(8,128)S(1)} %get-tuple-element.12.near, bf16[128,2048]{1,0:T(8,128)(2,1)S(1)} %get-tuple-element.13.gate, ...), custom_call_target="tpu_custom_call" | custom-call | flops 10000000 | bytes 5000000 | tf_op jit(solution)/shard_map/join/pallas_call | solution.py:454
  71.9 16.8 %all-gather = f32[4,1,128]{2,1,0:T(1,128)S(1)} all-gather(f32[1,1,128]{2,1,0:T(1,128)S(1)} %bitcast.20), channel_id=1, replica_groups=mesh['ch'=4,'gr'=16,'gc'=8] {'ch'}, dimensions={0}, use_global_device_ids=true | all-gather | bytes 2560 | tf_op jit(solution)/shard_map/all_gather | solution.py:455
  88.6 0.0 copy-done.3
  88.7 0.9 %scale.1 = bf16[128,2048]{1,0:T(8,128)(2,1)} custom-call(f32[4,128]{1,0:T(4,128)S(1)} %bitcast.19, f32[128,2048]{1,0:T(8,128)S(1)} %get-tuple-element.16.gated, f32[1,2048]{1,0:T(1,128)S(1)} %bitcast.18), custom_call_target="tpu_custom_call" | custom-call | flops 1000000 | bytes 2000000 | tf_op jit(solution)/shard_map/scale/pallas_call | solution.py:466
  (3 shorter events, 0.1 us)
Async XLA Ops:
  0.0 26.1 %copy-start.4 = (s32[8]{0:T(128)S(1)}, s32[8]{0:T(128)}, u32[]{:S(2)}) copy-start(s32[8]{0:T(128)} %lengths.5) | copy-start | bytes 100
  0.0 26.1 %copy-start.1 = (f32[16,2048]{1,0:T(8,128)S(1)}, f32[16,2048]{1,0:T(8,128)}, u32[]{:S(2)}) copy-start(f32[16,2048]{1,0:T(8,128)} %decay.3) | copy-start | bytes 393220
  0.0 26.2 %copy-start = (f32[3,7,2048]{2,1,0:T(8,128)S(1)}, f32[3,7,2048]{2,1,0:T(8,128)}, u32[]{:S(2)}) copy-start(f32[3,7,2048]{2,1,0:T(8,128)} %taps.3) | copy-start | bytes 516100
  0.0 26.2 %copy-start.2 = (f32[16,2048]{1,0:T(8,128)S(1)}, f32[16,2048]{1,0:T(8,128)}, u32[]{:S(2)}) copy-start(f32[16,2048]{1,0:T(8,128)} %residue.3) | copy-start | bytes 393220
  5.7 35.0 %all-to-all-start = ((bf16[128,2,384]{2,1,0:T(2,128)(2,1)}), bf16[128,2,384]{2,1,0:T(2,128)(2,1)S(1)}, u32[]{:S(2)}, u32[]{:S(2)}) async-start(bf16[128,2,384]{2,1,0:T(2,128)(2,1)} %reshape.28), calls=%async_computation | async-start | bytes 393216 | tf_op jit(solution)/shard_map/all_to_all | solution.py:353
  42.4 46.2 %copy-start.3 = (f32[2048]{0:T(1024)S(1)}, f32[2048]{0:T(1024)}, u32[]{:S(2)}) copy-start(f32[2048]{0:T(1024)} %param.11) | copy-start | bytes 24580

commit v7 on v5

--- a/solution.py
+++ b/solution.py
@@ -11,6 +11,7 @@
 LANES = 128
 TAPS = 7
 HEAD = TAPS - 1
+HALF = HEAD // 2
 SUB = 8
 VMEM_LIMIT = 12 * 1024 * 1024
 
@@ -47,14 +48,34 @@
 
 
 def fill_shifts(shifts, lengths, first_token):
-    tokens = shifts.shape[1]
+    count, tokens = shifts.shape
     row = rows_of((tokens, tokens))
     column = rows_of((tokens, tokens), 1)
     position = row + first_token
     reach = position - doc_start(lengths, position)
-    for i in range(1, TAPS):
+    for i in range(1, count // tokens + 1):
         hit = (column == row - i) & (reach >= i)
         shifts[(i - 1) * tokens : i * tokens, :] = jnp.where(hit, 1.0, 0.0).astype(jnp.bfloat16)
+
+
+def mixed_conv(shifts, masks, padded_x, x, taps):
+    tokens, width = x.shape
+    moved = jnp.dot(shifts[0 : HALF * tokens, :], x, preferred_element_type=jnp.float32)
+    found = []
+    for g in range(width // LANES):
+        mine = slice(g * LANES, (g + 1) * LANES)
+        values = x[:, mine].astype(jnp.float32)
+        padded_x[g, SUB : SUB + tokens, :] = values
+        total = values * taps(0)[:, mine]
+        for i in range(1, TAPS):
+            if i <= HALF:
+                term = moved[(i - 1) * tokens : i * tokens, mine] * taps(i)[:, mine]
+            else:
+                at = (i - HALF - 1) * tokens
+                term = padded_x[g, SUB - i : SUB - i + tokens, :] * taps(i)[:, mine] * masks[at : at + tokens, :]
+            total = total + term
+        found.append(total)
+    return jnp.concatenate(found, axis=1).astype(jnp.bfloat16)
 
 
 def product_of(first, third):
@@ -62,7 +83,9 @@
     return jnp.where(rows_of(product.shape) >= HEAD, product, 0.0).astype(jnp.bfloat16)
 
 
-def front_body(lengths_hbm, here, feats_hbm, taps_hbm, decay_hbm, msg, stage, feats, tail, taps, decay, shifts, lengths, sems):
+def front_body(
+    lengths_hbm, here, feats_hbm, taps_hbm, decay_hbm, msg, stage, feats, tail, taps, decay, shifts, masks, wide, lengths, sems
+):
     pair, tokens, channels = feats.shape
     modes = decay.shape[0]
     groups = channels // LANES
@@ -83,13 +106,22 @@
     used = states + 5 * HEAD * groups
     if used < stage.shape[0]:
         stage[used:, :] = jnp.zeros((stage.shape[0] - used, LANES), jnp.float32)
+    wide[:, :, 0:SUB, :] = jnp.zeros((pair, groups, SUB, LANES), jnp.float32)
     counted.wait()
     fill_shifts(shifts, lengths, here[0] * tokens)
+    row = rows_of((tokens, LANES))
+    position = row + here[0] * tokens
+    reach = jnp.minimum(position - doc_start(lengths, position), row)
+    for i in range(HALF + 1, TAPS):
+        at = (i - HALF - 1) * tokens
+        masks[at : at + tokens, :] = jnp.where(reach >= i, 1.0, 0.0)
     tapped.wait()
     found = []
     for k in range(pair):
         branches[k].wait()
-        found.append(short_conv(shifts[...], feats[k], lambda i, k=k: taps[2 * k, i : i + 1, :]))
+        found.append(
+            mixed_conv(shifts, masks, wide.at[k], feats[k], lambda i, k=k: taps[2 * k, i : i + 1, :])
+        )
     values = product_of(*found).astype(jnp.float32)
     for copy in others:
         copy.wait()
@@ -393,7 +425,9 @@
             vmem((2 * SUB, channels), bf16),
             vmem(short_taps.shape, f32),
             vmem(decay.shape, f32),
-            vmem((HEAD * tokens, tokens), bf16),
+            vmem((HALF * tokens, tokens), bf16),
+            vmem(((HEAD - HALF) * tokens, LANES), f32),
+            vmem((2, groups, SUB + tokens, LANES), f32),
             pltpu.SMEM(doc_lengths.shape, jnp.int32),
             pltpu.SemaphoreType.DMA((6,)),
         ],

time: 89.5 us -> 89.3 us (level)
  no operation moved by 1% of the time
where the time goes in v7:
time: 89.3 us; the launch traced here: 89 us
  blocking collectives  40.3 us (45%)
  Pallas kernels  21.4 us (24%)
  starting transfers between devices  20.4 us (23%)
  waiting for transfers between devices  5.84 us (7%)
    all_to_all x1, blocking collectives, exchange(): lax.all_to_all(block.reshape(blocks, 2, width // 2), ('gr', 'gc'), split_...  24 us
    all_to_all x1, starting transfers between devices, exchange(): lax.all_to_all(block.reshape(blocks, 2, width // 2), ('gr', 'gc'), split_...  20.4 us
    all_gather x1, blocking collectives, per_device(): energy = lax.all_gather(energy, 'ch', tiled=True)  16.3 us
    pallas_call x1, Pallas kernels, per_device(): local(doc_lengths, here, far(features), short_taps, decay, residue)  11.2 us
    all_to_all x1, waiting for transfers between devices, exchange(): lax.all_to_all(block.reshape(blocks, 2, width // 2), ('gr', 'gc'), split_...  5.84 us
    pallas_call x1, Pallas kernels, per_device(): front(far(doc_lengths), here, far(features), far(short_taps), far(decay))[0]  4.78 us
    pallas_call x1, Pallas kernels, per_device(): join(doc_lengths, here, given, near, gate, edge, decay, residue, short_taps)  2.89 us
  transfers between devices with their start and end apart: 1, of which 1 were waited for; matrix products, arithmetic and copies ran while one was open for 0% of the time, Pallas kernels for 13%

profile of v7, /device:TPU:1, one launch (start us, length us, event | category | flops | bytes accessed | tf_op | source)
XLA Modules:
  0.0 89.0 jit_solution(10947043580269744284)
XLA Ops:
  0.0 0.0 copy-start.4
  0.0 0.0 copy-start.1
  0.0 0.0 copy-start
  0.0 0.0 copy-start.2
  0.0 4.8 %front.1 = bf16[128,768]{1,0:T(8,128)(2,1)S(1)} custom-call(s32[8]{0:T(128)} %lengths.5, s32[1]{0:T(128)} %bitcast.here, bf16[3,128,2048]{2,1,0:T(8,128)(2,1)} %feats_hbm.3, f32[3,7,2048]{2,1,0:T(8,128)} %taps.3, f32[16,2048]{1,0:T(8,128)} %decay.3), custom_call_target="tpu_custom_call" | custom-call | flops 10000000 | bytes 4000000 | tf_op jit(solution)/shard_map/front/pallas_call | solution.py:438
  4.8 0.7 reshape.19
  5.5 20.4 %all-to-all-start = ((bf16[128,2,384]{2,1,0:T(2,128)(2,1)}), bf16[128,2,384]{2,1,0:T(2,128)(2,1)S(1)}, u32[]{:S(2)}, u32[]{:S(2)}) async-start(bf16[128,2,384]{2,1,0:T(2,128)(2,1)} %reshape.19), calls=%async_computation | async-start | bytes 393216 | tf_op jit(solution)/shard_map/all_to_all | solution.py:381
  25.9 0.0 copy-done.4
  26.0 0.0 copy-done.1
  26.0 0.0 copy-done
  26.0 0.0 copy-done.2
  26.0 11.2 %local.1 = (bf16[128,2048]{1,0:T(8,128)(2,1)S(1)}, f32[128,2048]{1,0:T(8,128)S(1)}, f32[8,2048]{1,0:T(8,128)S(1)}, f32[1360,128]{1,0:T(8,128)S(1)}) custom-call(s32[8]{0:T(128)S(1)} %copy-done.4, s32[1]{0:T(128)} %bitcast.here, bf16[3,128,2048]{2,1,0:T(8,128)(2,1)} %feats_hbm.3, f32[3,7,2048]{2,1,0:T(8,128)S(1)} %copy-done, f32[16,2048]{1,0:T(8,128)S(1)} %copy-done.1, ...), custom_call_target="tpu_custom_call" | custom-call | flops 100000000 | bytes 8000000 | tf_op jit(solution)/shard_map/local/pallas_call | solution.py:460
  37.2 5.8 %all-to-all-done = bf16[128,2,384]{2,1,0:T(2,128)(2,1)S(1)} async-done(((bf16[128,2,384]{2,1,0:T(2,128)(2,1)}), bf16[128,2,384]{2,1,0:T(2,128)(2,1)S(1)}, u32[]{:S(2)}, u32[]{:S(2)}) %all-to-all-start) | async-done | bytes 196640 | tf_op jit(solution)/shard_map/all_to_all | solution.py:381
  43.0 1.6 %owner.1 = bf16[128,512]{1,0:T(8,128)(2,1)S(1)} custom-call(s32[8]{0:T(128)S(1)} %copy-done.4, bf16[128,768]{1,0:T(8,128)(2,1)S(1)} %bitcast.8, f32[1360,128]{1,0:T(8,128)S(1)} %get-tuple-element.11.owned), custom_call_target="tpu_custom_call" | custom-call | flops 1000000 | bytes 1000000 | tf_op jit(solution)/shard_map/owner/pallas_call | solution.py:470
  44.7 0.0 copy-start.3
  44.7 24.0 %all_to_all.10 = bf16[128,2,256]{2,1,0:T(2,128)(2,1)S(1)} all-to-all(bf16[128,2,256]{2,1,0:T(2,128)(2,1)S(1)} %reshape.21), channel_id=1, replica_groups=mesh['ch'=4,'gr'=16,'gc'=8] {'gr','gc'}, dimensions={0} | all-to-all | bytes 262144 | tf_op jit(solution)/shard_map/all_to_all | solution.py:381
  68.8 2.9 %join.1 = (f32[128,2048]{1,0:T(8,128)S(1)}, f32[1,128]{1,0:T(1,128)S(1)}) custom-call(s32[8]{0:T(128)S(1)} %copy-done.4, s32[1]{0:T(128)} %bitcast.here, bf16[128,512]{1,0:T(8,128)(2,1)S(1)} %bitcast.9, f32[128,2048]{1,0:T(8,128)S(1)} %get-tuple-element.12.near, bf16[128,2048]{1,0:T(8,128)(2,1)S(1)} %get-tuple-element.13.gate, ...), custom_call_target="tpu_custom_call" | custom-call | flops 10000000 | bytes 5000000 | tf_op jit(solution)/shard_map/join/pallas_call | solution.py:481
  71.6 16.3 %all-gather = f32[4,1,128]{2,1,0:T(1,128)S(1)} all-gather(f32[1,1,128]{2,1,0:T(1,128)S(1)} %bitcast.12), channel_id=1, replica_groups=mesh['ch'=4,'gr'=16,'gc'=8] {'ch'}, dimensions={0}, use_global_device_ids=true | all-gather | bytes 2560 | tf_op jit(solution)/shard_map/all_gather | solution.py:482
  87.9 0.0 copy-done.3
  87.9 0.9 %scale.1 = bf16[128,2048]{1,0:T(8,128)(2,1)} custom-call(f32[4,128]{1,0:T(4,128)S(1)} %bitcast.11, f32[128,2048]{1,0:T(8,128)S(1)} %get-tuple-element.16.gated, f32[1,2048]{1,0:T(1,128)S(1)} %bitcast.10), custom_call_target="tpu_custom_call" | custom-call | flops 1000000 | bytes 2000000 | tf_op jit(solution)/shard_map/scale/pallas_call | solution.py:493
  (3 shorter events, 0.1 us)
Async XLA Ops:
  0.0 25.9 %copy-start.4 = (s32[8]{0:T(128)S(1)}, s32[8]{0:T(128)}, u32[]{:S(2)}) copy-start(s32[8]{0:T(128)} %lengths.5) | copy-start | bytes 100
  0.0 26.0 %copy-start.1 = (f32[16,2048]{1,0:T(8,128)S(1)}, f32[16,2048]{1,0:T(8,128)}, u32[]{:S(2)}) copy-start(f32[16,2048]{1,0:T(8,128)} %decay.3) | copy-start | bytes 393220
  0.0 26.0 %copy-start = (f32[3,7,2048]{2,1,0:T(8,128)S(1)}, f32[3,7,2048]{2,1,0:T(8,128)}, u32[]{:S(2)}) copy-start(f32[3,7,2048]{2,1,0:T(8,128)} %taps.3) | copy-start | bytes 516100
  0.0 26.0 %copy-start.2 = (f32[16,2048]{1,0:T(8,128)S(1)}, f32[16,2048]{1,0:T(8,128)}, u32[]{:S(2)}) copy-start(f32[16,2048]{1,0:T(8,128)} %residue.3) | copy-start | bytes 393220
  5.5 37.5 %all-to-all-start = ((bf16[128,2,384]{2,1,0:T(2,128)(2,1)}), bf16[128,2,384]{2,1,0:T(2,128)(2,1)S(1)}, u32[]{:S(2)}, u32[]{:S(2)}) async-start(bf16[128,2,384]{2,1,0:T(2,128)(2,1)} %reshape.19), calls=%async_computation | async-start | bytes 393216 | tf_op jit(solution)/shard_map/all_to_all | solution.py:381
  44.7 43.3 %copy-start.3 = (f32[2048]{0:T(1024)S(1)}, f32[2048]{0:T(1024)}, u32[]{:S(2)}) copy-start(f32[2048]{0:T(1024)} %param.11) | copy-start | bytes 24580
